TPU v7x, 32 devices: a whole 2x2x4 slice. The times are simulated.
32 devices in a mesh: bins: 4 (over z), chan: 4 (over y, x), seqs: 2 (over core).
Axes of the slice: x: 2, y: 2, z: 4, core: 2. Of those that a mesh axis runs over, the one named last changes fastest.
Arguments:
- inputs: bfloat16 [8, 1024, 768], P('seqs', 'bins'), may hold values from -30 to 30
- valid_bins: int32 [8, 1024], P('seqs', 'bins'), may hold values from 0 to 1, as said below
- cotangent: bfloat16 [8, 1024, 768], P('seqs', 'bins'), may hold values from -6 to 6
- conv1_weight: float32 [2304, 384], P(None, 'chan'), may hold values from -0.125 to 0.125
- conv1_momentum: float32 [2304, 384], P(None, 'chan'), may hold values from -1280 to 1280
- conv2_weight: float32 [384, 768], P('chan'), may hold values from -0.625 to 0.625
- conv2_momentum: float32 [384, 768], P('chan'), may hold values from -320 to 320
- norm1_params: float32 [2, 768], replicated, may hold values from -1 to 2, as said below
- norm1_momentum: float32 [2, 768], replicated, may hold values from -112 to 112
- norm2_params: float32 [2, 384], P(None, 'chan'), may hold values from -1 to 2, as said below
- norm2_momentum: float32 [2, 384], P(None, 'chan'), may hold values from -128 to 128
Outputs:
- output: bfloat16 [8, 1024, 768], P('seqs', 'bins')
- input_grad: float32 [8, 1024, 768], P('seqs', 'bins')
- conv1_moment: float32 [2304, 384], P(None, 'chan')
- conv1_new: float32 [2304, 384], P(None, 'chan')
- conv1_low: bfloat16 [2304, 384], P(None, 'chan')
- conv2_moment: float32 [384, 768], P('chan')
- conv2_new: float32 [384, 768], P('chan')
- conv2_low: bfloat16 [384, 768], P('chan')
- norm1_moment: float32 [2, 768], replicated
- norm1_new: float32 [2, 768], replicated
- norm2_moment: float32 [2, 384], P(None, 'chan')
- norm2_new: float32 [2, 384], P(None, 'chan')
Inputs may be any that keep to these rules, and one draw needn't show every extreme that they name: `valid_bins`: 1 marks a valid bin; the first bin of every sequence is valid. `norm1_params`: gains lie in 0.6 to 1.6. `norm2_params`: gains lie in 0.6 to 1.6.
All inputs are finite; a program needn't handle non-finite values.
Results may differ from a plain program's by a relative error of at most 0.0078.
Values may be sent and summed in bfloat16 or wider, within the bound.
No kernel may reach another device: no remote copies, remote signals or barrier semaphores. Data moves between devices by JAX's collectives and lax.ppermute only.
A program may use at most 64 MiB of HBM per device.

v0:
```python
import math

import jax
import jax.numpy as jnp
from jax import lax
from jax.sharding import PartitionSpec as P

DILATION_STEP = 28
NS_ITERS = 5


NORM_EPSILON = 0.001
GUARD_EPSILON = 1e-07
MOMENT_CONV = 0.95
RATE_CONV = 0.3
MOMENT_NORM = 0.9
RATE_NORM = 0.001
NEWTON_A = 3.4445
NEWTON_B = -4.775
NEWTON_C = 2.0315


def extended(cells, sides, width):
    for axis, dim in sides:
        count = lax.axis_size(axis)
        ends = count - 1
        head = lax.slice_in_dim(cells, 0, width, axis=dim)
        tail = lax.slice_in_dim(cells, cells.shape[dim] - width, cells.shape[dim], axis=dim)
        cells = jnp.concatenate(
            [
                lax.ppermute(tail, axis, [(i, (i + 1) % count) for i in range(ends)]),
                cells,
                lax.ppermute(head, axis, [((i + 1) % count, i) for i in range(ends)]),
            ],
            axis=dim,
        )
    return cells


def smooth(value):
    return value * jax.nn.sigmoid(1.702 * value)


def smooth_slope(value):
    sigma = jax.nn.sigmoid(1.702 * value)
    return sigma + 1.702 * value * sigma * (1.0 - sigma)


def gram_owned(row_block, first_flag):
    local_gram = jnp.einsum("rh,rk->hk", row_block, row_block, precision=lax.Precision.HIGHEST)
    grams = lax.psum(
        jnp.stack([first_flag * local_gram, (1.0 - first_flag) * local_gram]), ("bins", "seqs")
    )
    return first_flag * grams[0] + (1.0 - first_flag) * grams[1]


def orthogonal_rows(row_block, first_flag):
    gram = gram_owned(row_block, first_flag)
    scale = jnp.sqrt(jnp.trace(gram)) + GUARD_EPSILON
    row_block = row_block / scale
    gram = gram / (scale * scale)
    for sweep_no in range(NS_ITERS):
        squared = jnp.dot(gram, gram, precision=lax.Precision.HIGHEST)
        polynomial = NEWTON_B * gram + NEWTON_C * squared
        row_block = NEWTON_A * row_block + jnp.dot(
            row_block, polynomial, precision=lax.Precision.HIGHEST
        )
        if sweep_no < NS_ITERS - 1:
            gram = gram_owned(row_block, first_flag)
    return row_block


def shards(
    inputs,
    valid_bins,
    cotangent,
    conv1_weight,
    conv1_momentum,
    conv2_weight,
    conv2_momentum,
    norm1_params,
    norm1_momentum,
    norm2_params,
    norm2_momentum,
):
    local_sequences, local_bins, chan_width = inputs.shape
    row_count = local_sequences * local_bins
    local_hidden = conv1_weight.shape[1]
    kernel_tap_count = conv1_weight.shape[0] // chan_width
    flat_input = inputs.astype(jnp.float32).reshape(row_count, chan_width)
    valid_col = valid_bins.astype(jnp.float32).reshape(row_count, 1)
    first_sum, first_sq, counted = lax.psum(
        (
            jnp.sum(valid_col * flat_input, axis=0),
            jnp.sum(valid_col * flat_input * flat_input, axis=0),
            jnp.sum(valid_col),
        ),
        ("bins", "seqs"),
    )
    mean_one = first_sum / counted
    rstd_one = lax.rsqrt(first_sq / counted - mean_one * mean_one + NORM_EPSILON)
    norm_one = (flat_input - mean_one) * rstd_one
    pre_one = norm1_params[0] * norm_one + norm1_params[1]
    activated_reduced = (
        smooth(pre_one).astype(jnp.bfloat16).reshape(local_sequences, local_bins, chan_width)
    )
    padded_input = extended(activated_reduced, (("bins", 1),), DILATION_STEP)
    column_stack = jnp.concatenate(
        [
            padded_input[
                :,
                kernel_tap_index * DILATION_STEP : kernel_tap_index * DILATION_STEP + local_bins,
                :,
            ]
            for kernel_tap_index in range(kernel_tap_count)
        ],
        axis=2,
    )
    column_stack = column_stack.reshape(row_count, kernel_tap_count * chan_width)
    conv_low = conv1_weight.astype(jnp.bfloat16)
    hidden = jnp.dot(column_stack, conv_low, preferred_element_type=jnp.float32)
    second_sum, second_sq = lax.psum(
        (jnp.sum(valid_col * hidden, axis=0), jnp.sum(valid_col * hidden * hidden, axis=0)),
        ("bins", "seqs"),
    )
    mean_two = second_sum / counted
    rstd_two = lax.rsqrt(second_sq / counted - mean_two * mean_two + NORM_EPSILON)
    norm_two = (hidden - mean_two) * rstd_two
    pre_two = norm2_params[0] * norm_two + norm2_params[1]
    mixed_low = smooth(pre_two).astype(jnp.bfloat16)
    out_low = conv2_weight.astype(jnp.bfloat16)
    branch_out = lax.psum(jnp.dot(mixed_low, out_low, preferred_element_type=jnp.float32), "chan")
    output = (flat_input + branch_out).astype(jnp.bfloat16).reshape(inputs.shape)
    upstream = cotangent.reshape(row_count, chan_width)
    grad_second = jnp.einsum("rh,rc->hc", mixed_low, upstream, preferred_element_type=jnp.float32)
    grad_mixed = jnp.einsum("rc,hc->rh", upstream, out_low, preferred_element_type=jnp.float32)
    grad_pre_two = grad_mixed * smooth_slope(pre_two)
    gain_two, shift_two = lax.psum(
        (jnp.sum(grad_pre_two * norm_two, axis=0), jnp.sum(grad_pre_two, axis=0)), ("bins", "seqs")
    )
    hidden_gradient = (
        rstd_two
        * norm2_params[0]
        * (grad_pre_two - valid_col / counted * (shift_two + norm_two * gain_two))
    ).astype(jnp.bfloat16)
    grad_first = jnp.einsum(
        "rk,rh->kh", column_stack, hidden_gradient, preferred_element_type=jnp.float32
    )
    padded_gradient = extended(
        hidden_gradient.reshape(local_sequences, local_bins, local_hidden),
        (("bins", 1),),
        DILATION_STEP,
    )
    back_columns = jnp.concatenate(
        [
            padded_gradient[
                :,
                (kernel_tap_count - 1 - kernel_tap_index)
                * DILATION_STEP : (kernel_tap_count - 1 - kernel_tap_index)
                * DILATION_STEP
                + local_bins,
                :,
            ]
            for kernel_tap_index in range(kernel_tap_count)
        ],
        axis=2,
    )
    back_columns = back_columns.reshape(row_count, kernel_tap_count * local_hidden)
    back_weight = (
        conv_low.reshape(kernel_tap_count, chan_width, local_hidden)
        .transpose(0, 2, 1)
        .reshape(kernel_tap_count * local_hidden, chan_width)
    )
    grad_act = lax.psum(
        jnp.dot(back_columns, back_weight, preferred_element_type=jnp.float32), "chan"
    )
    grad_pre_one = grad_act * smooth_slope(pre_one)
    gain_one, shift_one = lax.psum(
        (jnp.sum(grad_pre_one * norm_one, axis=0), jnp.sum(grad_pre_one, axis=0)), ("bins", "seqs")
    )
    input_grad = upstream.astype(jnp.float32) + rstd_one * norm1_params[0] * (
        grad_pre_one - valid_col / counted * (shift_one + norm_one * gain_one)
    )
    input_grad = input_grad.reshape(inputs.shape)
    norm1_moment = MOMENT_NORM * norm1_momentum + jnp.stack([gain_one, shift_one])
    norm1_new = norm1_params - RATE_NORM * norm1_moment
    norm2_moment = MOMENT_NORM * norm2_momentum + jnp.stack([gain_two, shift_two])
    norm2_new = norm2_params - RATE_NORM * norm2_moment
    split_rows = conv1_weight.shape[0]
    local_grads = jnp.concatenate([grad_first, grad_second.T], axis=0)
    summed_rows = lax.psum_scatter(local_grads, ("bins", "seqs"), scatter_dimension=0, tiled=True)
    owned_count = summed_rows.shape[0]
    row_start = lax.axis_index(("bins", "seqs")) * owned_count
    old_moment = lax.dynamic_slice_in_dim(
        jnp.concatenate([conv1_momentum, conv2_momentum.T], axis=0), row_start, owned_count, 0
    )
    old_weight = lax.dynamic_slice_in_dim(
        jnp.concatenate([conv1_weight, conv2_weight.T], axis=0), row_start, owned_count, 0
    )
    moment_rows = MOMENT_CONV * old_moment + summed_rows
    full_rows = lax.all_gather(moment_rows, "chan", axis=1, tiled=True)
    hid_full = full_rows.shape[1]
    first_flag = (row_start < split_rows).astype(jnp.float32)
    orthogonal = orthogonal_rows(full_rows, first_flag)
    own_cols = lax.dynamic_slice_in_dim(
        orthogonal, lax.axis_index("chan") * local_hidden, local_hidden, 1
    )
    rate_first = RATE_CONV * math.sqrt(max(1.0, split_rows / hid_full))
    rate_second = RATE_CONV * math.sqrt(max(1.0, chan_width / hid_full))
    row_rate = first_flag * rate_first + (1.0 - first_flag) * rate_second
    weight_rows = old_weight - row_rate * own_cols
    moment_all, weight_all = (
        lax.all_gather(moment_rows, ("bins", "seqs"), axis=0, tiled=True),
        lax.all_gather(weight_rows, ("bins", "seqs"), axis=0, tiled=True),
    )
    conv1_moment = moment_all[:split_rows]
    conv1_new = weight_all[:split_rows]
    conv2_moment = moment_all[split_rows:].T
    conv2_new = weight_all[split_rows:].T
    return (
        output,
        input_grad,
        conv1_moment,
        conv1_new,
        conv1_new.astype(jnp.bfloat16),
        conv2_moment,
        conv2_new,
        conv2_new.astype(jnp.bfloat16),
        norm1_moment,
        norm1_new,
        norm2_moment,
        norm2_new,
    )


def solution(mesh):
    placed = (
        P("seqs", "bins", None),
        P("seqs", "bins"),
        P("seqs", "bins", None),
        P(None, "chan"),
        P(None, "chan"),
        P("chan", None),
        P("chan", None),
        P(),
        P(),
        P(None, "chan"),
        P(None, "chan"),
    )
    return jax.shard_map(
        shards,
        mesh=mesh,
        in_specs=placed,
        out_specs=(
            P("seqs", "bins", None),
            P("seqs", "bins", None),
            P(None, "chan"),
            P(None, "chan"),
            P(None, "chan"),
            P("chan", None),
            P("chan", None),
            P("chan", None),
            P(),
            P(),
            P(None, "chan"),
            P(None, "chan"),
        ),
        check_vma=False,
    )
```

profile of v0, /device:TPU:0, one launch (start us, length us, event | category | flops | bytes accessed | tf_op | source)
XLA Modules:
  0.0 659.2 jit_solution(17708659539189322500)
XLA Ops:
  7.2 0.8 convert_bitcast_fusion
  8.0 1.3 convert_reduce_fusion
  9.3 0.8 slice_reduce_fusion.1
  10.1 2.0 fusion
  12.1 19.2 %all-reduce.3 = (f32[768]{0:T(1024)S(1)}, f32[]{:T(128)}, f32[768]{0:T(1024)S(1)}) all-reduce(f32[768]{0:T(1024)S(1)} %get-tuple-element.15, f32[]{:T(128)} %convert_reduce_fusion, f32[768]{0:T(1024)S(1)} %get-tuple-element.14), channel_id=1, replica_groups=mesh['bins'=4,'chan'=4,'seqs'=2] {'bins','seqs'}, use_global_device_ids=true, to_apply=%region_1.0 | all-reduce | flops 1537 | bytes 12296 | tf_op jit(solution)/shard_map/psum | solution.py:92
  32.6 2.6 fusion.10
  35.3 1.3 collective-permute-start
  36.6 1.3 collective-permute-start.1
  38.6 1.1 collective-permute-done
  39.7 4.4 collective-permute-done.1
  44.6 2.3 fusion.55
  46.9 13.6 %all-reduce.2 = (f32[96]{0:T(128)S(1)}, f32[96]{0:T(128)S(1)}) all-reduce(f32[96]{0:T(128)S(1)} %get-tuple-element.17, f32[96]{0:T(128)S(1)} %get-tuple-element.16), channel_id=1, replica_groups=mesh['bins'=4,'chan'=4,'seqs'=2] {'bins','seqs'}, use_global_device_ids=true, to_apply=%region_7.0 | all-reduce | flops 192 | bytes 1536 | tf_op jit(solution)/shard_map/psum | solution.py:122
  60.5 0.8 fusion.80
  61.3 2.6 convolution_bitcast_fusion
  64.0 1.5 fusion.82
  65.4 13.6 %all-reduce.1 = (f32[96]{0:T(128)S(1)}, f32[96]{0:T(128)S(1)}) all-reduce(f32[96]{0:T(128)S(1)} %get-tuple-element.19, f32[96]{0:T(128)S(1)} %get-tuple-element.18), channel_id=1, replica_groups=mesh['bins'=4,'chan'=4,'seqs'=2] {'bins','seqs'}, use_global_device_ids=true, to_apply=%region_14.0 | all-reduce | flops 192 | bytes 1536 | tf_op jit(solution)/shard_map/psum | solution.py:138
  79.0 1.2 multiply_convert_fusion
  80.2 2.5 fusion.24
  82.8 1.1 pad_maximum_fusion.5
  84.0 31.0 %reduce-scatter.2.cloned.1.call-done = f32[384,96]{0,1:T(8,128)} async-done(((f32[3072,96]{0,1:T(8,128)}), f32[384,96]{0,1:T(8,128)}) %reduce-scatter.2.cloned.1.call-update) | async-done | bytes 147472 | tf_op jit(solution)/shard_map/reduce_scatter | solution.py:191
  115.0 0.9 fusion.70
  115.9 10.6 %all_gather.10 = f32[384,384]{0,1:T(8,128)S(1)} all-gather(f32[384,96]{0,1:T(8,128)S(1)} %fusion.70), channel_id=1, replica_groups=mesh['bins'=4,'chan'=4,'seqs'=2] {'chan'}, dimensions={1}, use_global_device_ids=true | all-gather | bytes 737280 | tf_op jit(solution)/shard_map/all_gather | solution.py:201
  126.5 1.3 multiply_bitcast_fusion.9
  127.8 1.1 pad_maximum_fusion.6
  129.0 57.5 %all-reduce.12.cloned.1.call-done = f32[2,384,384]{2,1,0:T(8,128)} async-done(((f32[2,384,384]{2,1,0:T(8,128)}), f32[2,384,384]{2,1,0:T(8,128)}) %all-reduce.12.cloned.1.call-update) | async-done | bytes 1179664 | tf_op jit(solution)/shard_map/psum | solution.py:51
  186.5 1.9 fusion.47
  189.0 3.7 fusion.26
  192.7 1.3 convolution_add_fusion.3
  194.0 1.3 multiply_bitcast_fusion.7
  195.3 1.1 pad_maximum_fusion.7
  196.7 58.5 %all-reduce.14.cloned.1.call-done = f32[2,384,384]{2,1,0:T(8,128)} async-done(((f32[2,384,384]{2,1,0:T(8,128)}), f32[2,384,384]{2,1,0:T(8,128)}) %all-reduce.14.cloned.1.call-update) | async-done | bytes 1179664 | tf_op jit(solution)/shard_map/psum | solution.py:51
  255.2 3.6 fusion.27
  258.8 1.3 convolution_add_fusion.2
  260.1 1.3 multiply_bitcast_fusion.5
  261.4 1.1 pad_maximum_fusion.8
  262.6 58.6 %all-reduce.16.cloned.1.call-done = f32[2,384,384]{2,1,0:T(8,128)} async-done(((f32[2,384,384]{2,1,0:T(8,128)}), f32[2,384,384]{2,1,0:T(8,128)}) %all-reduce.16.cloned.1.call-update) | async-done | bytes 1179664 | tf_op jit(solution)/shard_map/psum | solution.py:51
  321.2 3.6 fusion.28
  324.8 1.3 convolution_add_fusion.1
  326.1 1.3 multiply_bitcast_fusion.3
  327.4 1.1 pad_maximum_fusion.9
  328.8 58.4 %all-reduce.18.cloned.1.call-done = f32[2,384,384]{2,1,0:T(8,128)} async-done(((f32[2,384,384]{2,1,0:T(8,128)}), f32[2,384,384]{2,1,0:T(8,128)}) %all-reduce.18.cloned.1.call-update) | async-done | bytes 1179664 | tf_op jit(solution)/shard_map/psum | solution.py:51
  387.2 3.6 fusion.29
  390.8 1.3 convolution_add_fusion
  392.1 1.3 multiply_bitcast_fusion.1
  393.4 1.1 pad_maximum_fusion.10
  394.6 0.7 all-gather.3.cloned.1.call-update
  395.8 1.3 collective-permute-start.2
  397.1 4.6 collective-permute-start.3
  401.7 2.4 fusion.74
  404.1 1.3 collective-permute-done.3
  405.9 2.7 fusion.36
  408.7 44.6 %all-reduce.20.cloned.1.call-done = f32[2,384,384]{2,1,0:T(8,128)} async-done(((f32[2,384,384]{2,1,0:T(8,128)}), f32[2,384,384]{2,1,0:T(8,128)}) %all-reduce.20.cloned.1.call-update) | async-done | bytes 1179664 | tf_op jit(solution)/shard_map/psum | solution.py:51
  453.3 3.4 fusion.30
  456.8 1.4 fusion.87
  458.1 0.7 fusion.67
  459.5 17.7 %all-gather.3.cloned.1.call-done = f32[3072,96]{0,1:T(8,128)} async-done(((f32[384,96]{0,1:T(8,128)}), f32[3072,96]{0,1:T(8,128)}) %all-gather.3.cloned.1.call-update) | async-done | bytes 1179664 | tf_op jit(solution)/shard_map/all_gather | solution.py:213
  477.2 2.1 slice.114
  479.3 1.7 slice_bitcast_fusion.1
  481.0 138.9 %all-reduce.22.cloned.1.call-done = (f32[1024,768]{1,0:T(8,128)}, f32[1024,768]{1,0:T(8,128)}) async-done(((f32[1024,768]{1,0:T(8,128)}, f32[1024,768]{1,0:T(8,128)}), (f32[1024,768]{1,0:T(8,128)}, f32[1024,768]{1,0:T(8,128)})) %all-reduce.22.cloned.1.call-update) | async-done | bytes 6291472 | tf_op jit(solution)/shard_map/psum | solution.py:132
  619.9 4.5 fusion.81
  624.4 16.8 %all-reduce = (f32[768]{0:T(1024)S(1)}, f32[768]{0:T(1024)S(1)}) all-reduce(f32[768]{0:T(1024)S(1)} %get-tuple-element.13, f32[768]{0:T(1024)S(1)} %get-tuple-element.12), channel_id=1, replica_groups=mesh['bins'=4,'chan'=4,'seqs'=2] {'bins','seqs'}, use_global_device_ids=true, to_apply=%region_19.0 | all-reduce | flops 1536 | bytes 12288 | tf_op jit(solution)/shard_map/psum | solution.py:178
  641.9 6.8 %fusion.23 = (f32[1024,768]{1,0:T(8,128)}, bf16[1024,768]{1,0:T(8,128)(2,1)}) fusion(f32[1024,768]{1,0:T(8,128)} %get-tuple-element.43, bf16[4,256,768]{2,1,0:T(8,128)(2,1)S(1)} %copy-done, f32[768]{0:T(1024)S(1)} %get-tuple-element.22, f32[768]{0:T(1024)S(1)} %get-tuple-element.23, f32[1024]{0:T(1024)S(1)} %broadcast_divide_fusion, ...), kind=kLoop, calls=%fused_computation.29 | loop fusion | flops 9437184 | bytes 14175232 | tf_op jit(solution)/shard_map/add | solution.py:181
  648.6 2.3 fusion.84
  651.0 1.7 fusion.83
  (70 shorter events, 5.6 us)
Async XLA Ops:
  7.2 30.7 %copy-start.1 = (f32[2304,96]{0,1:T(8,128)S(1)}, f32[2304,96]{0,1:T(8,128)}, u32[]{:S(2)}) copy-start(f32[2304,96]{0,1:T(8,128)} %param.14) | copy-start | bytes 2654212
  7.2 107.8 %reduce-scatter.2.cloned.1.call-start = ((), (), s32[]{:S(2)}) async-start(), calls=%async_computation.1 | async-start | bytes 1327104 | tf_op jit(solution)/shard_map/reduce_scatter | solution.py:191
  10.1 28.5 %copy-start.13 = (f32[2,96]{1,0:T(2,128)S(1)}, f32[2,96]{1,0:T(2,128)}, u32[]{:S(2)}) copy-start(f32[2,96]{1,0:T(2,128)} %param.20) | copy-start | bytes 2308
  35.3 4.5 collective-permute-start
  36.6 7.6 %collective-permute-start.1 = (bf16[4,28,768]{2,1,0:T(8,128)(2,1)S(1)}, bf16[4,28,768]{2,1,0:T(8,128)(2,1)S(1)}, u32[]{:S(2)}, u32[]{:S(2)}) collective-permute-start(bf16[4,28,768]{2,1,0:T(8,128)(2,1)S(1)} %get-tuple-element.52), channel_id=1, source_target_pairs={{8,0},{16,8},{24,16},{9,1},{17,9},{25,17},{10,2},{18,10},{26,18},{... | collective-permute-start | bytes 516104 | tf_op jit(solution)/shard_map/ppermute | solution.py:33
  44.6 2.3 copy-start.2
  44.6 2.3 copy-start.3
  60.5 3.4 copy-start.4
  60.5 3.4 copy-start.6
  80.2 2.5 copy-start.10
  82.8 32.2 %copy-start.9 = (f32[2304,96]{0,1:T(8,128)S(1)}, f32[2304,96]{0,1:T(8,128)}, u32[]{:S(2)}) copy-start(f32[2304,96]{0,1:T(8,128)} %param.15) | copy-start | bytes 2654212
  82.8 32.2 %copy-start.11 = (f32[96,768]{1,0:T(8,128)S(1)}, f32[96,768]{1,0:T(8,128)}, u32[]{:S(2)}) copy-start(f32[96,768]{1,0:T(8,128)} %param.17) | copy-start | bytes 884740
  83.9 102.5 %all-reduce.12.cloned.1.call-start = ((), (), s32[]{:S(2)}) async-start(), calls=%async_computation.3 | async-start | bytes 2359296 | tf_op jit(solution)/shard_map/psum | solution.py:51
  115.9 13.0 %copy-start.5 = (f32[384,96]{0,1:T(8,128)}, f32[384,96]{0,1:T(8,128)S(1)}, u32[]{:S(2)}) copy-start(f32[384,96]{0,1:T(8,128)S(1)} %fusion.70) | copy-start | bytes 442372
  128.9 126.3 %all-reduce.14.cloned.1.call-start = ((), (), s32[]{:S(2)}) async-start(), calls=%async_computation.4 | async-start | bytes 2359296 | tf_op jit(solution)/shard_map/psum | solution.py:51
  196.4 124.7 %all-reduce.16.cloned.1.call-start = ((), (), s32[]{:S(2)}) async-start(), calls=%async_computation.5 | async-start | bytes 2359296 | tf_op jit(solution)/shard_map/psum | solution.py:51
  262.5 124.7 %all-reduce.18.cloned.1.call-start = ((), (), s32[]{:S(2)}) async-start(), calls=%async_computation.6 | async-start | bytes 2359296 | tf_op jit(solution)/shard_map/psum | solution.py:51
  328.5 124.8 %all-reduce.20.cloned.1.call-start = ((), (), s32[]{:S(2)}) async-start(), calls=%async_computation.7 | async-start | bytes 2359296 | tf_op jit(solution)/shard_map/psum | solution.py:51
  393.4 8.3 %copy-start.7 = (f32[96,768]{1,0:T(8,128)S(1)}, f32[96,768]{1,0:T(8,128)}, u32[]{:S(2)}) copy-start(f32[96,768]{1,0:T(8,128)} %param.16) | copy-start | bytes 884740
  394.5 82.6 %all-gather.3.cloned.1.call-start = ((), (), s32[]{:S(2)}) async-start(), calls=%async_computation.2 | async-start | bytes 1327104 | tf_op jit(solution)/shard_map/all_gather | solution.py:213
  395.3 224.6 %all-reduce.22.cloned.1.call-start = ((), (), s32[]{:S(2)}) async-start(), calls=%async_computation.9 | async-start | bytes 12582912 | tf_op jit(solution)/shard_map/psum | solution.py:132
  395.8 8.3 %collective-permute-start.2 = (bf16[4,28,96]{1,0,2:T(4,128)(2,1)S(1)}, bf16[4,28,96]{1,0,2:T(4,128)(2,1)S(1)}, u32[]{:S(2)}, u32[]{:S(2)}) collective-permute-start(bf16[4,28,96]{1,0,2:T(4,128)(2,1)S(1)} %get-tuple-element.65), channel_id=1, source_target_pairs={{8,0},{16,8},{24,16},{9,1},{17,9},{25,17},{10,2},{18,10},{26,18},{... | collective-permute-start | bytes 64520 | tf_op jit(solution)/shard_map/ppermute | solution.py:33
  397.1 8.3 %collective-permute-start.3 = (bf16[4,28,96]{1,0,2:T(4,128)(2,1)S(1)}, bf16[4,28,96]{1,0,2:T(4,128)(2,1)S(1)}, u32[]{:S(2)}, u32[]{:S(2)}) collective-permute-start(bf16[4,28,96]{1,0,2:T(4,128)(2,1)S(1)} %get-tuple-element.66), channel_id=1, source_target_pairs={{0,8},{8,16},{16,24},{1,9},{9,17},{17,25},{2,10},{10,18},{18,26},{... | collective-permute-start | bytes 64520 | tf_op jit(solution)/shard_map/ppermute | solution.py:31
  408.6 49.5 %copy-start.8 = (f32[96,768]{1,0:T(8,128)S(1)}, f32[96,768]{1,0:T(8,128)}, u32[]{:S(2)}) copy-start(f32[96,768]{1,0:T(8,128)} %param.16) | copy-start | bytes 884740
  408.6 50.3 %copy-start.15 = (f32[2,96]{1,0:T(2,128)S(1)}, f32[2,96]{1,0:T(2,128)}, u32[]{:S(2)}) copy-start(f32[2,96]{1,0:T(2,128)} %param.21) | copy-start | bytes 2308
  408.6 240.0 %all-gather.5.cloned.1.call-start = ((), (), s32[]{:S(2)}) async-start(), calls=%async_computation.8 | async-start | bytes 1327104 | tf_op jit(solution)/shard_map/all_gather | solution.py:214
  456.8 163.1 %copy-start = (bf16[4,256,768]{2,1,0:T(8,128)(2,1)S(1)}, bf16[4,256,768]{2,1,0:T(8,128)(2,1)}, u32[]{:S(2)}) copy-start(bf16[4,256,768]{2,1,0:T(8,128)(2,1)} %param.11) | copy-start | bytes 4718596
  619.9 21.4 %copy-start.12 = (f32[2,768]{1,0:T(2,128)S(1)}, f32[2,768]{1,0:T(2,128)}, u32[]{:S(2)}) copy-start(f32[2,768]{1,0:T(2,128)} %param.18) | copy-start | bytes 18436
  619.9 21.4 %copy-start.14 = (f32[2,768]{1,0:T(2,128)S(1)}, f32[2,768]{1,0:T(2,128)}, u32[]{:S(2)}) copy-start(f32[2,768]{1,0:T(2,128)} %param.19) | copy-start | bytes 18436
Sparse Core Ops, SparseCore 0:
  84.1 30.8 reduce-scatter.1
  129.0 57.3 all-reduce.11
  196.6 58.5 all-reduce.13
  262.6 58.4 all-reduce.15
  328.6 58.4 all-reduce.17
  394.7 58.6 all-reduce.19
  455.5 21.6 all-gather.2
  481.3 138.5 all-reduce.21
  622.0 22.9 all-gather.4
where the time goes:
time: 660 us; the launch traced here: 659 us
  waiting for transfers between devices  473 us (72%)
  blocking collectives  73.8 us (11%)
  matrix products  44.9 us (7%)
  other arithmetic  38.2 us (6%)
  between operations  15.1 us (2%)
  starting transfers between devices  9.21 us (1%)
    psum x5, waiting for transfers between devices, gram_owned(): lax.psum(jnp.stack([first_flag * local_gram, (1.0 - first_flag) * local_g...  278 us
    psum x1, waiting for transfers between devices, shards(): lax.psum(jnp.dot(mixed_low, out_low, preferred_element_type=jnp.float32),...  139 us
    reduce_scatter x1, waiting for transfers between devices, shards(): lax.psum_scatter(local_grads, ('bins', 'seqs'), scatter_dimension=0, tile...  31 us
    psum x1, blocking collectives, shards(): lax.psum((jnp.sum(valid_col * flat_input, axis=0), jnp.sum(valid_col * fl...  19.2 us
    dot_general x5, matrix products, orthogonal_rows(): squared = jnp.dot(gram, gram, precision=lax.Precision.HIGHEST)  17.9 us
    all_gather x1, waiting for transfers between devices, shards(): lax.all_gather(moment_rows, ('bins', 'seqs'), axis=0, tiled=True)  17.7 us
    psum x1, blocking collectives, shards(): lax.psum((jnp.sum(grad_pre_one * norm_one, axis=0), jnp.sum(grad_pre_one,...  16.8 us
    psum x1, blocking collectives, shards(): lax.psum((jnp.sum(valid_col * hidden, axis=0), jnp.sum(valid_col * hidden...  13.6 us
  transfers between devices with their start and end apart: 13, of which 11 were waited for; matrix products, arithmetic and copies ran while one was open for 4% of the time, Pallas kernels for 0%

commit v1 on v0

v1 whole, which is shorter than its diff:
```python
import functools
import math

import jax
import jax.numpy as jnp
from jax import lax
from jax.experimental import pallas as pl
from jax.experimental.pallas import tpu as pltpu
from jax.sharding import PartitionSpec as P

DILATION_STEP = 28
NS_ITERS = 5

NORM_EPSILON = 0.001
GUARD_EPSILON = 1e-07
MOMENT_CONV = 0.95
RATE_CONV = 0.3
MOMENT_NORM = 0.9
RATE_NORM = 0.001
NEWTON_A = 3.4445
NEWTON_B = -4.775
NEWTON_C = 2.0315
HALO = 32
LANES = 128
F32 = jnp.float32
BF16 = jnp.bfloat16


def flipped(value, axis, mask):
    count = lax.axis_size(axis)
    return lax.ppermute(value, axis, [(i, i ^ mask) for i in range(count)])


def short(axis):
    return lax.axis_size(axis) == 4


def partners(value, axis):
    rest = [flipped(value, axis, mask) for mask in range(lax.axis_size(axis) - 1, 0, -1)]
    return [value] + rest[::-1]


def summed(parts):
    parts = list(parts)
    while len(parts) > 1:
        parts = [parts[i] + parts[i + 1] for i in range(0, len(parts), 2)]
    return parts[0]


def terms(value):
    return partners(value, "bins") if short("bins") else [lax.psum(value, "bins")]


def doubled(value, mask=1, ahead=()):
    if not short("bins"):
        return lax.psum(value, "bins"), ahead
    while mask < lax.axis_size("bins"):
        if 2 * mask == lax.axis_size("bins"):
            value, ahead = tied(value, ahead)
        value = value + flipped(value, "bins", mask)
        mask *= 2
    return value, ahead


def tied(*values):
    return lax.optimization_barrier(values)


def exchanged(first, second):
    count, cores = lax.axis_size("bins"), lax.axis_size("seqs")

    def to(start):
        pairs = []
        for z in range(count):
            other = z + 1 if (z - start) % 2 == 0 else z - 1
            for core in range(cores):
                inside = 0 <= other < count
                target = other * cores + core if inside else z * cores + (core ^ 1)
                pairs.append((z * cores + core, target))
        return pairs

    return [lax.ppermute(value, ("bins", "seqs"), to(start)) for start, value in enumerate((first, second))]


def even(axis):
    return lax.rem(lax.axis_index(axis), 2) == 0


def dot(left, right):
    return lax.dot_general(left, right, (((1,), (0,)), ((), ())), preferred_element_type=F32)


def dot_rows(left, right):
    return lax.dot_general(left, right, (((1,), (1,)), ((), ())), preferred_element_type=F32)


def dot_columns(left, right):
    return lax.dot_general(left, right, (((0,), (0,)), ((), ())), preferred_element_type=F32)


def sigmoid(value):
    return 0.5 + 0.5 * jnp.tanh(0.851 * value)


def mask_of(valid_ref, i):
    valid = valid_ref[i : i + 1, :].astype(F32)
    return jnp.broadcast_to(valid, (LANES, valid.shape[1])).T


def rows_of(*parts):
    width = parts[0].shape[1]
    return jnp.concatenate(list(parts) + [jnp.zeros((8 - len(parts), width), F32)], axis=0)


def put_edges(first_ref, second_ref, i, head, tail):
    to_next = even("bins")
    first_ref[i] = jnp.where(to_next, tail, head)
    second_ref[i] = jnp.where(to_next, head, tail)


def inner(count):
    place = lax.axis_index("bins")
    return (place > 0).astype(F32), (place < count - 1).astype(F32)


def edges_of(first_ref, second_ref, i):
    to_next = even("bins")
    first, second = first_ref[i].astype(F32), second_ref[i].astype(F32)
    return jnp.where(to_next, second, first), jnp.where(to_next, first, second)


def stats_kernel(x_any, valid_any, sums_ref, first_ref, second_ref, x_ref, valid_ref, arrived):
    seqs, bins, width = x_ref.shape
    copies = [pltpu.make_async_copy(valid_any, valid_ref, arrived.at[seqs])] + [
        pltpu.make_async_copy(x_any.at[i], x_ref.at[i], arrived.at[i]) for i in range(seqs)
    ]
    for copy in copies:
        copy.start()
    copies.pop(0).wait()
    first = second = count = 0.0
    for i in range(seqs):
        mask = mask_of(valid_ref, i)
        copies[i].wait()
        kept = x_ref[i].astype(F32) * jnp.concatenate([mask] * (width // LANES), axis=1)
        first += jnp.sum(kept, axis=0, keepdims=True)
        second += jnp.sum(kept * kept, axis=0, keepdims=True)
        count += jnp.sum(mask, axis=0, keepdims=True)
        put_edges(first_ref, second_ref, i, x_ref[i, :HALO, :], x_ref[i, bins - HALO :, :])
    sums_ref[...] = rows_of(first, second, jnp.concatenate([count] * (width // LANES), axis=1))


def prep_kernel(after_ref, *refs):
    out_ref, other_ref, first_ref, second_ref, *held = refs[4:12]
    arrived = refs[12]
    copies = [
        pltpu.make_async_copy(ref, buffer, arrived.at[i])
        for i, (ref, buffer) in enumerate(zip(refs[:4], held))
    ]
    for copy in copies:
        copy.start()
    weight_one, weight_two, momentum_one, momentum_two = held
    split, width = weight_one.shape[1], weight_two.shape[1]
    half = (split + width) // 2

    def put(ref, start, value):
        ref[:, start : start + value.shape[1]] = value.astype(BF16)

    def put_two(start, value):
        high, low = split2(value)
        put(out_ref, half + start, high)
        put(out_ref, 2 * half + start, low)

    def put_low(ref):
        put(ref, 0, weight_one[:, :half])

    def put_high(ref):
        put(ref, 0, weight_one[:, half:])
        put(ref, split - half, weight_two[...])

    for copy in copies[:2]:
        copy.wait()
    own = weight_one.shape[0]
    for k in range(split // width):
        first_ref[k * LANES : k * LANES + own, :] = weight_one[:, k * width : (k + 1) * width].astype(BF16)
        first_ref[k * LANES + own : (k + 1) * LANES, :] = jnp.zeros((LANES - own, width), BF16)
    second_ref[:own, :] = weight_two[...].astype(BF16)
    second_ref[own:, :] = jnp.zeros((LANES - own, width), BF16)
    for copy in copies[2:]:
        copy.wait()
    side = lax.axis_index("seqs")

    @pl.when(side == 0)
    def _():
        put_low(out_ref)
        put_high(other_ref)
        put_two(0, momentum_one[:, :half])

    @pl.when(side != 0)
    def _():
        put_high(out_ref)
        put_low(other_ref)
        put_two(0, momentum_one[:, half:])
        put_two(split - half, momentum_two[...])


def conv_kernel(parts, count, *refs):
    pieces = refs[:parts]
    (x_ref, first_ref, second_ref, params_ref, low_ref, valid_ref,
     act_ref, hidden_ref, sums_ref, stat_ref, wide_ref) = refs[parts:]
    seqs, bins, width = x_ref.shape
    taps = low_ref.shape[0] // LANES
    sums = summed([p[...] for p in pieces])
    counted = sums[2:3]
    mean = sums[0:1] / counted
    rstd = lax.rsqrt(sums[1:2] / counted - mean * mean + NORM_EPSILON)
    gain = params_ref[0:1, :] * rstd
    bias = params_ref[1:2, :] - mean * gain
    stat_ref[...] = rows_of(mean, rstd, counted, gain, bias)
    first, last = inner(count)

    def activated(cells):
        value = cells.astype(F32) * gain + bias
        return value * sigmoid(value)

    total = squares = 0.0
    for i in range(seqs):
        before, after = edges_of(first_ref, second_ref, i)
        act_ref[i, :HALO, :] = (activated(before) * first).astype(BF16)
        act_ref[i, HALO : HALO + bins, :] = activated(x_ref[i]).astype(BF16)
        act_ref[i, HALO + bins :, :] = (activated(after) * last).astype(BF16)
        wide_ref[...] = dot_rows(act_ref[i], low_ref[...])
        hidden = 0.0
        for k in range(taps):
            start = HALO + (k - taps // 2) * DILATION_STEP
            hidden += wide_ref[start : start + bins, k * LANES : (k + 1) * LANES]
        hidden_ref[i * bins : (i + 1) * bins, :] = hidden
        kept = mask_of(valid_ref, i) * hidden
        total += jnp.sum(kept, axis=0, keepdims=True)
        squares += jnp.sum(kept * hidden, axis=0, keepdims=True)
    sums_ref[...] = rows_of(total, squares)


def back_kernel(upstream_ref, low_ref, out_ref):
    out_ref[...] = dot_rows(upstream_ref[...], low_ref[...])


def mix_kernel(parts, *refs):
    pieces = refs[:parts]
    (stat_one_ref, params_ref, hidden_ref, back_ref,
     mixed_ref, grad_ref, sums_ref, stat_ref) = refs[parts:]
    sums = summed([p[...] for p in pieces])
    counted = stat_one_ref[2:3, :LANES]
    mean = sums[0:1] / counted
    rstd = lax.rsqrt(sums[1:2] / counted - mean * mean + NORM_EPSILON)
    stat_ref[...] = rows_of(mean, rstd, counted)
    norm = (hidden_ref[...] - mean) * rstd
    value = params_ref[0:1, :] * norm + params_ref[1:2, :]
    sigma = sigmoid(value)
    mixed = value * sigma
    mixed_ref[...] = mixed.astype(BF16)
    grad = back_ref[...] * (sigma + 1.702 * mixed * (1.0 - sigma))
    grad_ref[...] = grad
    sums_ref[...] = rows_of(
        jnp.sum(grad * norm, axis=0, keepdims=True), jnp.sum(grad, axis=0, keepdims=True)
    )


def grads_kernel(parts, *refs):
    pieces = refs[:parts]
    (stat_ref, params_ref, hidden_ref, grad_ref, valid_ref, mixed_ref, act_ref, upstream_ref,
     keep_ref, give_ref, grad_low_ref, first_ref, second_ref, shift_ref) = refs[parts:]
    seqs, padded, width = act_ref.shape
    bins = padded - 2 * HALO
    taps = shift_ref.shape[1] // LANES
    own = keep_ref.shape[0]
    sums = summed([p[...] for p in pieces])
    mean, rstd, counted = stat_ref[0:1, :], stat_ref[1:2, :], stat_ref[2:3, :]
    mask = jnp.concatenate([mask_of(valid_ref, i) for i in range(seqs)], axis=0)
    norm = (hidden_ref[...] - mean) * rstd
    grad = rstd * params_ref[0:1, :] * (
        grad_ref[...] - mask / counted * (sums[1:2] + norm * sums[0:1])
    )
    low = grad.astype(BF16)
    grad = low.astype(F32)
    grad_low_ref[...] = low
    for i in range(seqs):
        part = grad[i * bins : (i + 1) * bins, :]
        put_edges(
            first_ref, second_ref, i, part[:HALO].astype(BF16), part[bins - HALO :].astype(BF16)
        )
        for k in range(taps):
            start = HALO + (k - taps // 2) * DILATION_STEP
            lanes = slice(k * LANES, (k + 1) * LANES)
            base = i * padded
            shift_ref[base : base + start, lanes] = jnp.zeros((start, LANES), F32)
            shift_ref[base + start : base + start + bins, lanes] = part
            shift_ref[base + start + bins : base + padded, lanes] = jnp.zeros(
                (padded - start - bins, LANES), F32
            )
    act = act_ref[...].reshape(seqs * padded, width)
    first = dot_columns(shift_ref[...].astype(BF16), act)
    second = dot_columns(mixed_ref[...], upstream_ref[...])
    both = [first[k * LANES : k * LANES + own, :] for k in range(taps)] + [second[:own, :]]
    count = len(both) // 2

    def put(ref, blocks):
        for k, block in enumerate(blocks):
            ref[:, k * width : (k + 1) * width] = block.astype(ref.dtype)

    side = lax.axis_index("seqs")

    @pl.when(side == 0)
    def _():
        put(keep_ref, both[:count])
        put(give_ref, both[count:])

    @pl.when(side != 0)
    def _():
        put(keep_ref, both[count:])
        put(give_ref, both[:count])


def pair_kernel(keep_ref, give_ref, first_ref, second_ref, *outs):
    place = lax.axis_index("bins")
    own, size = outs[0].shape
    for mask, out in enumerate(outs):
        columns = pl.ds(pl.multiple_of((place ^ mask) * size, LANES), size)
        out[:own, :] = (keep_ref[:, columns] + give_ref[:, columns].astype(F32)).astype(BF16)
    for out, edge in ((outs[1], first_ref), (outs[3], second_ref)):
        rows = edge[...].reshape(-1, LANES)
        depth = out.shape[0] - own
        for k in range(size // LANES):
            block = rows[k * depth : (k + 1) * depth]
            if block.shape[0] < depth:
                block = jnp.concatenate([block, jnp.zeros((depth - block.shape[0], LANES), BF16)], axis=0)
            out[own:, k * LANES : (k + 1) * LANES] = block


def add_kernel(*refs):
    chunks, (sum_ref, first_ref, second_ref) = refs[:4], refs[4:]
    own = sum_ref.shape[0]
    sum_ref[...] = summed([ref[:own, :].astype(F32) for ref in chunks]).astype(BF16)
    for chunk, edge in ((chunks[1], first_ref), (chunks[3], second_ref)):
        parts = [chunk[own:, k * LANES : (k + 1) * LANES] for k in range(chunk.shape[1] // LANES)]
        rows = jnp.concatenate(parts, axis=0)
        edge[...] = rows[: edge.shape[0] * edge.shape[1]].reshape(edge.shape)


def place_kernel(*refs):
    place = lax.axis_index("bins")
    size = refs[0].shape[1]
    for mask, ref in enumerate(refs[:-1]):
        columns = pl.ds(pl.multiple_of((place ^ mask) * size, LANES), size)
        refs[-1][:, columns] = ref[...]


def halves_kernel(one_ref, two_ref, first_ref, second_ref):
    middle = first_ref.shape[1]
    first_ref[...] = one_ref[:, :middle]
    second_ref[...] = two_ref[:, middle:]


def pack_kernel(*refs):
    own, half = refs[0].shape[0], refs[-1].shape[1]
    for j, ref in enumerate(refs[:-1]):
        refs[-1][j * own : (j + 1) * own, :] = ref[:, :half]


def both_kernel(mixed_ref, grad_ref, both_ref):
    rows = mixed_ref.shape[0]
    own = LANES // 4 * 3
    lane = lax.broadcasted_iota(jnp.int32, (rows, LANES), 1)
    moved = pltpu.roll(mixed_ref[...].astype(F32), own, 1)
    both_ref[:rows, :] = jnp.where(lane < own, grad_ref[...].astype(F32), moved).astype(BF16)
    both_ref[rows:, :] = jnp.where(
        lane[: rows // 2] < LANES // 2, moved[: rows // 2], pltpu.roll(moved[rows // 2 :], LANES // 2, 1)
    ).astype(BF16)


def edges_kernel(count, first_ref, second_ref, edges_ref):
    first, last = inner(count)
    for i in range(first_ref.shape[0]):
        before, after = edges_of(first_ref, second_ref, i)
        start = 2 * i * HALO
        edges_ref[start : start + HALO, :] = (before * first).astype(BF16)
        edges_ref[start + HALO : start + 2 * HALO, :] = (after * last).astype(BF16)


def fill_kernel(*refs):
    halves, (first_other, rest_other, weight_ref) = refs[:4], refs[4:]
    own = first_other.shape[0]
    count = len(halves)
    others = [first_other] + [rest_other.at[j * own : (j + 1) * own] for j in range(count - 1)]
    taps, _, width = weight_ref.shape
    step = taps // 2

    def put(low_refs, high_refs):
        for k in range(taps):
            column = k % step * width
            for j, ref in enumerate(low_refs if k < step else high_refs):
                weight_ref[k, j * LANES : j * LANES + own, :] = ref[:, column : column + width]
                weight_ref[k, j * LANES + own : (j + 1) * LANES, :] = jnp.zeros(
                    (LANES - own, width), BF16
                )

    side = lax.axis_index("seqs")

    @pl.when(side == 0)
    def _():
        put(halves, others)

    @pl.when(side != 0)
    def _():
        put(others, halves)


def branch_kernel(x_ref, weight_ref, *refs):
    blocks, output_ref = refs[:4], refs[4]
    seqs, bins, width = x_ref.shape
    rows = seqs * bins
    rest = LANES // 4
    lane = lax.broadcasted_iota(jnp.int32, (bins, LANES), 1)
    for i in range(seqs):
        mixed = []
        for block in blocks:
            start = rows + i * bins % (rows // 2)
            shift = rest + (LANES // 2 if i >= seqs // 2 else 0)
            mixed.append(
                jnp.where(
                    lane < rest,
                    pltpu.roll(block[i * bins : (i + 1) * bins, :].astype(F32), rest, 1),
                    pltpu.roll(block[start : start + bins, :].astype(F32), shift, 1),
                ).astype(BF16)
            )
        branch = dot(jnp.concatenate(mixed, axis=1), weight_ref[weight_ref.shape[0] - 1])
        output_ref[i] = (x_ref[i].astype(F32) + branch).astype(BF16)


def tail_kernel(x_ref, upstream_ref, stat_ref, weight_ref, *refs):
    blocks, edges, (grad_ref, sums_ref, wide_ref) = refs[:4], refs[4:8], refs[8:]
    seqs, bins, width = x_ref.shape
    taps = weight_ref.shape[0] - 1
    mean, rstd = stat_ref[0:1, :], stat_ref[1:2, :]
    gain, bias = stat_ref[3:4, :], stat_ref[4:5, :]
    first = second = 0.0
    for i in range(seqs):
        for j, block in enumerate(blocks):
            lanes = slice(j * LANES, (j + 1) * LANES)
            outer, start = edges[j], 2 * i * HALO
            wide_ref[:HALO, lanes] = outer[start : start + HALO, :].astype(F32)
            wide_ref[HALO : HALO + bins, lanes] = block[i * bins : (i + 1) * bins, :].astype(F32)
            wide_ref[HALO + bins :, lanes] = outer[start + HALO : start + 2 * HALO, :].astype(F32)
        x = x_ref[i].astype(F32)
        act = 0.0
        for k in range(taps):
            start = HALO - (k - taps // 2) * DILATION_STEP
            act += dot(wide_ref[start : start + bins, :].astype(BF16), weight_ref[k])
        value = x * gain + bias
        sigma = sigmoid(value)
        grad = act * (sigma + 1.702 * value * sigma * (1.0 - sigma))
        grad_ref[i] = upstream_ref[i].astype(F32) + gain * grad
        norm = (x - mean) * rstd
        first += jnp.sum(grad * norm, axis=0, keepdims=True)
        second += jnp.sum(grad, axis=0, keepdims=True)
    sums_ref[...] = rows_of(first, second)


def input_grad_kernel(start, total_ref, grad_ref, x_ref, stat_ref, valid_ref, *refs):
    out_ref, left = refs[-2:]
    width = x_ref.shape[2]
    sums = total_ref[...]
    mean, rstd, counted, gain = (stat_ref[k : k + 1, :] for k in range(4))
    slope = gain / counted * rstd * sums[0:1]
    level = gain / counted * sums[1:2] - mean * slope
    copies = []
    if start == 0:
        params_ref, momentum_ref, out_any, moment_any, new_any, moment_ref, new_ref, sems = refs[:8]
        moment = MOMENT_NORM * momentum_ref[...] + sums[:2]
        moment_ref[...] = moment
        new_ref[...] = params_ref[...] - RATE_NORM * moment
        copies = [
            pltpu.make_async_copy(moment_ref, moment_any, sems.at[0]),
            pltpu.make_async_copy(new_ref, new_any, sems.at[1]),
        ]
        for copy in copies:
            copy.start()
    else:
        out_any = refs[1]
    for i in range(out_ref.shape[0]):
        mask = jnp.concatenate([mask_of(valid_ref, start + i)] * (width // LANES), axis=1)
        out_ref[i] = grad_ref[start + i] - mask * (level + x_ref[start + i].astype(F32) * slope)
        copies.append(pltpu.make_async_copy(out_ref.at[i], out_any.at[start + i], left.at[i]))
        copies[-1].start()
    for copy in copies:
        copy.wait()


def split2(value):
    high = value.astype(BF16)
    return high, (value - high.astype(F32)).astype(BF16)


def split3(value):
    high, mid = split2(value)
    rest = value - high.astype(F32) - mid.astype(F32)
    return high, mid, rest.astype(BF16)


def triple(l1, l2, r1, r2):
    return dot(
        jnp.concatenate([l1, l1, l2], axis=1), jnp.concatenate([r1, r2, r1], axis=0)
    )


def product_fine(left, right):
    l1, l2, l3 = split3(left)
    r1, r2, r3 = split3(right)
    return dot(
        jnp.concatenate([l1, l1, l2, l2, l1, l3], axis=1),
        jnp.concatenate([r1, r2, r1, r2, r3, r1], axis=0),
    )


def gram_kernel(right, *refs):
    parameters, parts = refs[:5], refs[5:9]
    high_ref, low_ref, gram_ref = refs[9:]
    size, width = parts[0].shape
    half = width // 2
    base = half if right else 0
    for j, part in enumerate(parts):
        if j < 3:
            source = parameters[j][:, width:]
        else:
            source = jnp.concatenate([parameters[3][:, width:], parameters[4][...]], axis=1)
        momentum = (
            source[:, base : base + half].astype(F32)
            + source[:, width + base : width + base + half].astype(F32)
        )
        high, low = split2(MOMENT_CONV * momentum + part[:, base : base + half].astype(F32))
        high_ref[j * size : (j + 1) * size, :] = high
        low_ref[j * size : (j + 1) * size, :] = low
    high = high_ref[...]
    cross = dot_rows(high, low_ref[...])
    gram_ref[...] = dot_rows(high, high) + (cross + cross.T)


def newton_kernel(own, left_ref, right_ref, other_ref, factor_ref):
    first = (lax.axis_index("seqs") == 0).astype(F32)
    gram = right_ref[...] + first * (left_ref[...] + other_ref[...])
    size = gram.shape[0]
    diagonal = lax.broadcasted_iota(jnp.int32, (size, size), 0) == lax.broadcasted_iota(
        jnp.int32, (size, size), 1
    )
    scale = jnp.sqrt(jnp.sum(jnp.where(diagonal, gram, 0.0), keepdims=True)) + GUARD_EPSILON
    gram = gram / (scale * scale)
    ones = jnp.where(diagonal, NEWTON_A, 0.0)
    factor = None
    for sweep in range(NS_ITERS):
        if sweep == 0:
            g1, g2 = split2(gram)
            poly = ones + NEWTON_B * gram + NEWTON_C * triple(g1, g2, g1, g2)
            factor = poly[:own, :] / scale
            g1, g2 = split2(product_fine(gram, poly))
            gram = triple(g1, g2, *split2(poly))
            continue
        g1, g2 = split2(gram)
        f1, f2 = split2(factor)
        if sweep == NS_ITERS - 1:
            once = triple(f1, f2, g1, g2)
            factor = NEWTON_A * factor + NEWTON_B * once + NEWTON_C * triple(*split2(once), g1, g2)
            continue
        poly = ones + NEWTON_B * gram + NEWTON_C * triple(g1, g2, g1, g2)
        p1, p2 = split2(poly)
        both = triple(
            jnp.concatenate([g1, f1], axis=0), jnp.concatenate([g2, f2], axis=0), p1, p2
        )
        factor = both[size:, :]
        g1, g2 = split2(both[:size, :])
        gram = triple(g1, g2, p1, p2)
    factor_ref[...] = factor


def product_of(factor, high, low):
    f1, f2 = split2(factor)
    return (dot(f1, high) + (dot(f2, high) + dot(f1, low))).astype(BF16)


def right_kernel(own_ref, high_ref, low_ref, step_ref):
    step_ref[...] = product_of(own_ref[...], high_ref[...], low_ref[...])


def left_kernel(own_ref, other_ref, high_ref, low_ref, step_ref):
    factor = jnp.where(lax.axis_index("seqs") == 0, own_ref[...], other_ref[...])
    step_ref[...] = product_of(factor, high_ref[...], low_ref[...])


def halves_of(half_ref, other_ref, use):
    side = lax.axis_index("seqs")

    @pl.when(side == 0)
    def _():
        use(half_ref, other_ref)

    @pl.when(side != 0)
    def _():
        use(other_ref, half_ref)


def moment_kernel(half_ref, other_ref, one_ref, two_ref, moment_one, moment_two):
    half = half_ref.shape[1]
    split = one_ref.shape[1] - half

    def use(low_ref, high_ref):
        moment_one[:, :half] = MOMENT_CONV * one_ref[:, :half] + low_ref[...].astype(F32)
        moment_one[:, half:] = MOMENT_CONV * one_ref[:, half:] + high_ref[:, :split].astype(F32)
        moment_two[...] = MOMENT_CONV * two_ref[...] + high_ref[:, split:].astype(F32)

    halves_of(half_ref, other_ref, use)


def finish_kernel(rate_one, rate_two, left_ref, right_ref, left_other, right_other, one_ref, two_ref, *refs):
    outs, held, sems = refs[:4], refs[4:8], refs[8]
    new_one, low_one, new_two, low_two = held
    width = two_ref.shape[1]
    side = lax.axis_index("seqs")

    def sent(k, slot, columns):
        copy = pltpu.make_async_copy(held[k].at[:, columns], outs[k].at[:, columns], sems.at[slot])
        copy.start()
        return copy

    def use(blocks):
        copies = []
        for k, block in enumerate(blocks):
            last = k == len(blocks) - 1
            columns = slice(0, width) if last else slice(k * width, (k + 1) * width)
            new_ref, low_ref = (new_two, low_two) if last else (new_one, low_one)
            old = two_ref[...] if last else one_ref[:, columns]
            value = old - (rate_two if last else rate_one) * block[...].astype(F32)
            new_ref[:, columns] = value
            low_ref[:, columns] = value.astype(BF16)
            copies += [sent(2 * last, 2 * k, columns), sent(2 * last + 1, 2 * k + 1, columns)]
        for copy in copies:
            copy.wait()

    @pl.when(side == 0)
    def _():
        use([left_ref, right_ref, left_other, right_other])

    @pl.when(side != 0)
    def _():
        use([left_other, right_other, left_ref, right_ref])


def call(kernel, outs, args, name, flops, mebibytes, scratch=(), outside=(), outside_outs=(), aliases=None):
    specs = [
        pl.BlockSpec(memory_space=pltpu.HBM if i in outside else pltpu.VMEM) for i in range(len(args))
    ]
    operands = [
        pltpu.with_memory_space_constraint(v, pltpu.HBM) if i in outside else v
        for i, v in enumerate(args)
    ]
    outs = [jax.ShapeDtypeStruct(shape, dtype) for shape, dtype in outs]
    nbytes = sum(math.prod(v.shape) * v.dtype.itemsize for v in list(args) + outs)
    return pl.pallas_call(
        kernel,
        out_shape=tuple(outs),
        in_specs=specs,
        out_specs=tuple(
            pl.BlockSpec(memory_space=pltpu.HBM if i in outside_outs else pltpu.VMEM)
            for i in range(len(outs))
        ),
        scratch_shapes=list(scratch),
        input_output_aliases=aliases or {},
        compiler_params=pltpu.CompilerParams(vmem_limit_bytes=mebibytes * 2**20),
        cost_estimate=pl.CostEstimate(flops=flops, bytes_accessed=nbytes, transcendentals=0),
        name=name,
    )(*operands)


def shards(
    inputs,
    valid_bins,
    cotangent,
    conv1_weight,
    conv1_momentum,
    conv2_weight,
    conv2_momentum,
    norm1_params,
    norm1_momentum,
    norm2_params,
    norm2_momentum,
):
    seqs, bins, chan = inputs.shape
    rows = seqs * bins
    padded = bins + 2 * HALO
    own = conv1_weight.shape[1]
    taps = conv1_weight.shape[0] // chan
    conv1_rows = taps * chan
    all_rows = conv1_rows + chan
    half = all_rows // 2
    split = conv1_rows - half
    bins_count = lax.axis_size("bins")
    hid = own * lax.axis_size("chan")
    weight_t, momentum_t = conv1_weight.T, conv1_momentum.T

    sums, head, tail = call(
        stats_kernel,
        [((8, chan), F32), ((seqs, HALO, chan), BF16), ((seqs, HALO, chan), BF16)],
        [inputs, valid_bins], "stats", 5 * rows * chan, 10,
        [pltpu.VMEM(inputs.shape, BF16), pltpu.VMEM((seqs, bins), jnp.int32),
         pltpu.SemaphoreType.DMA((seqs + 1,))], (0, 1),
    )
    first, second = exchanged(head, tail)

    owned = [weight_t, conv2_weight, momentum_t, conv2_momentum]
    parameters, weights_other, low_one, low_two = call(
        prep_kernel,
        [((own, 3 * half), BF16), ((own, half), BF16), ((taps * LANES, chan), BF16), ((LANES, chan), BF16)],
        [sums] + owned, "prep", 6 * own * half, 12,
        [pltpu.VMEM(v.shape, F32) for v in owned] + [pltpu.SemaphoreType.DMA((4,))], (1, 2, 3, 4),
    )
    paired = sums + flipped(sums, "seqs", 1)
    paired, sent = tied(paired, parameters)
    parameters_one, parameters_two = flipped(sent, "chan", 1), flipped(sent, "chan", 2)
    if short("bins"):
        total = paired + flipped(paired, "bins", 1)
        total, first, second = tied(total, first, second)
        total = total + flipped(total, "bins", 2)
    else:
        total = lax.psum(paired, "bins")
    pieces = [total]

    act, hidden, sums, stat_one = call(
        functools.partial(conv_kernel, len(pieces), lax.axis_size("bins")),
        [((seqs, padded, chan), BF16), ((rows, LANES), F32), ((8, LANES), F32), ((8, chan), F32)],
        pieces + [inputs, first, second, norm1_params, low_one, valid_bins],
        "conv", 2 * seqs * padded * chan * taps * LANES, 14,
        [pltpu.VMEM((padded, taps * LANES), F32)],
    )
    upstream = cotangent.reshape(rows, chan)
    (back,) = call(
        back_kernel, [((rows, LANES), F32)], [upstream, low_two], "back", 2 * rows * chan * LANES, 6,
    )

    params_two = jnp.pad(norm2_params, ((0, 0), (0, LANES - own)))
    pieces = terms(sums + flipped(sums, "seqs", 1))
    pieces, parameters_one, parameters_two, back = tied(pieces, parameters_one, parameters_two, back)
    middle = 3 * half // 2
    first, second = call(
        halves_kernel, [((own, middle), BF16), ((own, middle), BF16)], [parameters_one, parameters_two],
        "halves", 1, 6,
    )
    parameters_three = [flipped(first, "chan", 2), flipped(second, "chan", 1)]
    mixed, grad, sums, stat_two = call(
        functools.partial(mix_kernel, len(pieces)),
        [((rows, LANES), BF16), ((rows, LANES), F32), ((8, LANES), F32), ((8, LANES), F32)],
        pieces + [stat_one, params_two, hidden, back], "mix", 30 * rows * LANES, 8,
    )
    total = sums + flipped(sums, "seqs", 1)
    pieces = terms(total)
    keep, give, grad_hidden, first, second = call(
        functools.partial(grads_kernel, len(pieces)),
        [((own, half), F32), ((own, half), BF16), ((rows, LANES), BF16),
         ((seqs, HALO, LANES), BF16), ((seqs, HALO, LANES), BF16)],
        pieces + [stat_two, params_two, hidden, grad, valid_bins, mixed, act, upstream],
        "grads", 2 * seqs * padded * chan * taps * LANES, 16,
        [pltpu.VMEM((seqs * padded, taps * LANES), F32)],
    )

    norm2_moment = MOMENT_NORM * norm2_momentum + summed(pieces)[:2, :own]
    norm2_new = norm2_params - RATE_NORM * norm2_moment

    taken = flipped(give, "seqs", 1)
    taken, parameters_three = tied(taken, parameters_three)
    (both,) = call(
        both_kernel, [((rows + rows // 2, LANES), BF16)], [mixed, grad_hidden], "both", 1, 6
    )
    both_one, both_two = flipped(both, "chan", 1), flipped(both, "chan", 2)
    parameters = [parameters, parameters_one, parameters_two] + parameters_three
    packed_from = parameters[1:4]
    if short("bins"):
        size = half // bins_count
        depth = -(-seqs * HALO * LANES // size // 16) * 16
        chunk, deep = ((own, size), BF16), ((own + depth, size), BF16)
        chunks = call(
            pair_kernel, [chunk, deep, chunk, deep], [keep, taken, first, second], "pair", own * half, 6
        )
        chunks = [
            c if m == 0 else flipped(c, "bins", m) for m, c in reversed(list(enumerate(chunks)))
        ][::-1]
        chunks, both_one, both_two = tied(chunks, both_one, both_two)
        edge = ((seqs, HALO, LANES), BF16)
        sum_half, first, second = call(add_kernel, [chunk, edge, edge], chunks, "add", own * half, 6)
        sum_half, sent, packed_from = tied(sum_half, both, packed_from)
    else:
        sum_half = keep + taken.astype(F32)
        first, second = exchanged(first, second)
        sent = both
    border = 2 * seqs * HALO
    (edges,) = call(
        functools.partial(edges_kernel, bins_count), [((border, LANES), BF16)], [first, second], "edges", 1, 4
    )
    both_three = flipped(sent, "chan", 3)
    (packed,) = call(pack_kernel, [((3 * own, half), BF16)], packed_from, "pack", 1, 8)
    weights_rest = flipped(packed, "seqs", 1)
    (filled,) = call(
        fill_kernel, [((taps + 1, 4 * LANES, chan), BF16)],
        parameters[:4] + [weights_other, weights_rest], "fill", 1, 12,
    )
    filled, edges = tied(filled, edges)
    edges = partners(edges, "chan")
    both = [both, both_one, both_two, both_three]
    if short("bins"):
        totals = partners(sum_half, "bins")
        totals, filled = tied(totals, filled)
        (grads_half,) = call(
            place_kernel, [((own, half), BF16)], totals, "place", own * half, 4,
        )
    else:
        grads_half = lax.psum(sum_half, "bins").astype(BF16)
    gathered = partners(grads_half, "chan")

    grad_one, sums = call(
        tail_kernel,
        [((seqs, bins, chan), F32), ((8, chan), F32)],
        [inputs, cotangent, stat_one, filled] + both + edges,
        "tail", 2 * rows * chan * taps * 4 * LANES, 18, [pltpu.VMEM((padded, 4 * LANES), F32)],
    )
    (output,) = call(
        branch_kernel, [((seqs, bins, chan), BF16)], [inputs, filled] + both, "branch",
        2 * rows * chan * 4 * LANES, 14,
    )
    sums_one = sums + flipped(sums, "seqs", 1)
    if short("bins"):
        sums_one = sums_one + flipped(sums_one, "bins", 1)
    grads_half, sums = tied(grads_half, sums)
    grads_other = flipped(grads_half, "seqs", 1)
    conv1_moment, conv2_moment = call(
        moment_kernel, [((own, conv1_rows), F32), ((own, chan), F32)],
        [grads_half, grads_other, momentum_t, conv2_momentum], "moment", 2 * own * all_rows, 12,
    )
    (
        gathered, output, grad_one, sums_one, norm2_moment, norm2_new, conv1_moment, conv2_moment
    ) = tied(
        gathered, output, grad_one, sums_one, norm2_moment, norm2_new, conv1_moment, conv2_moment
    )

    square, wide = ((hid, hid), F32), ((hid, half // 2), BF16)
    (high_left, low_left, gram_left), (high_right, low_right, gram_right) = [
        call(
            functools.partial(gram_kernel, right), [wide, wide, square], parameters + gathered,
            "gram_right" if right else "gram_left", 4 * hid * hid * half, 12,
        )
        for right in (False, True)
    ]
    gram_other = flipped(gram_left, "seqs", 1)
    (own_factor,) = call(
        functools.partial(newton_kernel, own), [((own, hid), F32)],
        [gram_left, gram_right, gram_other], "newton", 100 * hid**3, 14,
    )
    if short("bins"):
        last = flipped(sums_one, "bins", 2)
        own_factor, last = tied(own_factor, last)
        sums_one = sums_one + last
    else:
        sums_one = lax.psum(sums_one, "bins")
    other_factor = flipped(own_factor, "seqs", 1)
    quarter = ((own, half // 2), BF16)
    (right,) = call(right_kernel, [quarter], [own_factor, high_right, low_right], "right", 3 * own * hid * half, 8)
    field = [grad_one, inputs, stat_one, valid_bins]
    middle = seqs // 2
    buffer = [pltpu.VMEM((middle, bins, chan), F32), pltpu.SemaphoreType.DMA((middle,))]
    input_grad, norm1_moment, norm1_new = call(
        functools.partial(input_grad_kernel, 0),
        [((seqs, bins, chan), F32), ((2, chan), F32), ((2, chan), F32)],
        [sums_one] + field + [norm1_params, norm1_momentum], "input_grad", 5 * rows * chan, 16,
        [pltpu.VMEM((2, chan), F32), pltpu.VMEM((2, chan), F32), pltpu.SemaphoreType.DMA((2,))] + buffer,
        (), (0, 1, 2),
    )
    other_factor, input_grad = tied(other_factor, input_grad)
    (left,) = call(
        left_kernel, [quarter], [own_factor, other_factor, high_left, low_left], "left", 3 * own * hid * half, 8
    )
    step_other = [flipped(left, "seqs", 1), flipped(right, "seqs", 1)]
    (input_grad,) = call(
        functools.partial(input_grad_kernel, middle), [((seqs, bins, chan), F32)],
        [sums_one] + field + [input_grad], "input_grad_rest", 5 * rows * chan, 16,
        buffer, (5,), (0,), {5: 0},
    )
    conv1_new, conv1_low, conv2_new, conv2_low = call(
        functools.partial(
            finish_kernel,
            RATE_CONV * math.sqrt(max(1.0, conv1_rows / hid)),
            RATE_CONV * math.sqrt(max(1.0, chan / hid)),
        ),
        [((own, conv1_rows), F32), ((own, conv1_rows), BF16), ((own, chan), F32), ((own, chan), BF16)],
        [left, right] + step_other + [weight_t, conv2_weight], "finish", 2 * own * all_rows, 12,
        [pltpu.VMEM((own, conv1_rows), F32), pltpu.VMEM((own, conv1_rows), BF16),
         pltpu.VMEM((own, chan), F32), pltpu.VMEM((own, chan), BF16), pltpu.SemaphoreType.DMA((8,))],
        (), (0, 1, 2, 3),
    )
    return (
        output,
        input_grad,
        conv1_moment.T,
        conv1_new.T,
        conv1_low.T,
        conv2_moment,
        conv2_new,
        conv2_low,
        norm1_moment,
        norm1_new,
        norm2_moment,
        norm2_new,
    )


def solution(mesh):
    placed = (
        P("seqs", "bins", None),
        P("seqs", "bins"),
        P("seqs", "bins", None),
        P(None, "chan"),
        P(None, "chan"),
        P("chan", None),
        P("chan", None),
        P(),
        P(),
        P(None, "chan"),
        P(None, "chan"),
    )
    return jax.shard_map(
        shards,
        mesh=mesh,
        in_specs=placed,
        out_specs=(
            P("seqs", "bins", None),
            P("seqs", "bins", None),
            P(None, "chan"),
            P(None, "chan"),
            P(None, "chan"),
            P("chan", None),
            P("chan", None),
            P("chan", None),
            P(),
            P(),
            P(None, "chan"),
            P(None, "chan"),
        ),
        check_vma=False,
    )
```

time: 660 us -> 104 us (0.16)
  waiting for transfers between devices: 473 us -> 25.4 us
  blocking collectives: 73.8 us -> 0 us
  matrix products: 44.9 us -> 0 us
  other arithmetic: 38.2 us -> 0.61 us
  starting transfers between devices: 9.21 us -> 44.4 us
  Pallas kernels: 0 us -> 32.2 us
  between operations: 15.1 us -> 1.25 us
    psum x6 -> x0, waiting for transfers between devices: 416 us -> none  [the longest x5 278 us: gram_owned(): lax.psum(jnp.stack([first_flag * local_gram, (1.0 - first_flag) * local_g...]
    psum x4 -> x0, blocking collectives: 63.2 us -> none  [the longest x1 19.2 us: shards(): lax.psum((jnp.sum(valid_col * flat_input, axis=0), jnp.sum(valid_col * fl...]
    dot_general x21 -> x0, matrix products: 44.9 us -> none  [the longest x5 17.9 us: orthogonal_rows(): squared = jnp.dot(gram, gram, precision=lax.Precision.HIGHEST)]
    ppermute x4 -> x42, starting transfers between devices: 8.44 us -> 44.4 us  [the longest x40 42.8 us: flipped(): return lax.ppermute(value, axis, [(i, i ^ mask) for i in range(count)])]
    pallas_call x0 -> x25, Pallas kernels: none -> 32.2 us  [call(): pl.pallas_call(kernel, out_shape=tuple(outs), in_specs=specs, out_specs=t...]
    reduce_scatter x1 -> x0, waiting for transfers between devices: 31 us -> none  [shards(): lax.psum_scatter(local_grads, ('bins', 'seqs'), scatter_dimension=0, tile...]
    ppermute x4 -> x42, waiting for transfers between devices: 6.78 us -> 25.4 us  [the longest x40 25.4 us: flipped(): return lax.ppermute(value, axis, [(i, i ^ mask) for i in range(count)])]
    all_gather x2 -> x0, waiting for transfers between devices: 17.7 us -> none  [the longest x1 17.7 us: shards(): lax.all_gather(moment_rows, ('bins', 'seqs'), axis=0, tiled=True)]
  transfers between devices with their start and end apart: 13 -> 42, of which waited for: 11 -> 19; matrix products, arithmetic and copies ran while one was open for 4% -> 1% of each run, Pallas kernels for 0% -> 27%
where the time goes in v1:
time: 104 us
  starting transfers between devices  44.4 us (43%)
  Pallas kernels  32.2 us (31%)
  waiting for transfers between devices  25.4 us (24%)
  between operations  1.25 us (1%)
    ppermute x40, starting transfers between devices, flipped(): return lax.ppermute(value, axis, [(i, i ^ mask) for i in range(count)])  42.8 us
    pallas_call x25, Pallas kernels, call(): pl.pallas_call(kernel, out_shape=tuple(outs), in_specs=specs, out_specs=t...  32.2 us
    ppermute x40, waiting for transfers between devices, flipped(): return lax.ppermute(value, axis, [(i, i ^ mask) for i in range(count)])  25.4 us
  transfers between devices with their start and end apart: 42, of which 19 were waited for; matrix products, arithmetic and copies ran while one was open for 1% of the time, Pallas kernels for 27%

profile of v1, /device:TPU:0, one launch (start us, length us, event | category | flops | bytes accessed | tf_op | source)
XLA Modules:
  0.0 103.9 jit_solution(6475349770287356364)
XLA Ops:
  0.7 2.2 %stats.1 = (f32[8,768]{1,0:T(8,128)S(1)}, bf16[4,32,768]{2,1,0:T(8,128)(2,1)S(1)}, bf16[4,32,768]{2,1,0:T(8,128)(2,1)S(1)}) custom-call(bf16[4,256,768]{2,1,0:T(8,128)(2,1)} %x_ref.7, s32[4,256]{1,0:T(4,128)} %valid_ref.3), custom_call_target="tpu_custom_call" | custom-call | flops 3932160 | bytes 1994752 | tf_op jit(solution)/shard_map/stats/pallas_call | solution.py:665
  2.9 0.5 collective-permute-start
  3.4 1.8 %prep.1 = (bf16[96,4608]{1,0:T(8,128)(2,1)S(1)}, bf16[96,1536]{1,0:T(8,128)(2,1)S(1)}, bf16[384,768]{1,0:T(8,128)(2,1)S(1)}, bf16[128,768]{1,0:T(8,128)(2,1)S(1)}) custom-call(f32[8,768]{1,0:T(8,128)S(1)} %get-tuple-element.107.after_ref, f32[96,2304]{1,0:T(8,128)} %bitcast.10, f32[96,768]{1,0:T(8,128)} %two_ref.3, f32[96,2304]{1,0:T(8,128)} %bitcast.8, ...), custom_call_target="tpu_custom_call" | custom-call | flops 884736 | bytes 4349952 | tf_op jit(solution)/shard_map/prep/pallas_call | solution.py:665
  5.2 2.6 %collective-permute-start.10 = (bf16[96,4608]{1,0:T(8,128)(2,1)S(1)}, bf16[96,4608]{1,0:T(8,128)(2,1)S(1)}, u32[]{:S(2)}, u32[]{:S(2)}) collective-permute-start(bf16[96,4608]{1,0:T(8,128)(2,1)S(1)} %get-tuple-element.117.refs_0_), channel_id=1, source_target_pairs={{0,4},{2,6},{4,0},{6,2},{1,5},{3,7},{5,1},{7,3},{8,12},{10,14},{12... | collective-permute-start | bytes 2654216 | tf_op jit(solution)/shard_map/ppermute | solution.py:31
  7.8 1.5 %collective-permute-start.9 = (bf16[96,4608]{1,0:T(8,128)(2,1)S(1)}, bf16[96,4608]{1,0:T(8,128)(2,1)S(1)}, u32[]{:S(2)}, u32[]{:S(2)}) collective-permute-start(bf16[96,4608]{1,0:T(8,128)(2,1)S(1)} %get-tuple-element.117.refs_0_), channel_id=1, source_target_pairs={{0,2},{2,0},{4,6},{6,4},{1,3},{3,1},{5,7},{7,5},{8,10},{10,8},{12,... | collective-permute-start | bytes 2654216 | tf_op jit(solution)/shard_map/ppermute | solution.py:31
  9.3 1.6 %collective-permute-start.2 = (bf16[4,32,768]{2,1,0:T(8,128)(2,1)S(1)}, bf16[4,32,768]{2,1,0:T(8,128)(2,1)S(1)}, u32[]{:S(2)}, u32[]{:S(2)}) collective-permute-start(bf16[4,32,768]{2,1,0:T(8,128)(2,1)S(1)} %get-tuple-element.110), channel_id=1, source_target_pairs={{0,8},{1,9},{8,0},{9,1},{16,24},{17,25},{24,16},{25,17},{2,10},{3,... | collective-permute-start | bytes 589832 | tf_op jit(solution)/shard_map/ppermute | solution.py:82
  10.9 3.1 %collective-permute-start.1 = (f32[8,768]{1,0:T(8,128)S(1)}, f32[8,768]{1,0:T(8,128)S(1)}, u32[]{:S(2)}, u32[]{:S(2)}) collective-permute-start(f32[8,768]{1,0:T(8,128)S(1)} %add.39), channel_id=1, source_target_pairs={{0,8},{8,0},{16,24},{24,16},{1,9},{9,1},{17,25},{25,17},{2,10},{10... | collective-permute-start | bytes 73736 | tf_op jit(solution)/shard_map/ppermute | solution.py:31
  14.0 2.5 %collective-permute-done.1 = f32[8,768]{1,0:T(8,128)S(1)} collective-permute-done((f32[8,768]{1,0:T(8,128)S(1)}, f32[8,768]{1,0:T(8,128)S(1)}, u32[]{:S(2)}, u32[]{:S(2)}) %collective-permute-start.1) | collective-permute-done | bytes 24608 | tf_op jit(solution)/shard_map/ppermute | solution.py:31
  16.6 3.3 %collective-permute-start.4 = (f32[8,768]{1,0:T(8,128)S(1)}, f32[8,768]{1,0:T(8,128)S(1)}, u32[]{:S(2)}, u32[]{:S(2)}) collective-permute-start(f32[8,768]{1,0:T(8,128)S(1)} %add.40), channel_id=1, source_target_pairs={{0,16},{8,24},{16,0},{24,8},{1,17},{9,25},{17,1},{25,9},{2,18},{10... | collective-permute-start | bytes 73736 | tf_op jit(solution)/shard_map/ppermute | solution.py:31
  19.9 1.8 %collective-permute-done.4 = f32[8,768]{1,0:T(8,128)S(1)} collective-permute-done((f32[8,768]{1,0:T(8,128)S(1)}, f32[8,768]{1,0:T(8,128)S(1)}, u32[]{:S(2)}, u32[]{:S(2)}) %collective-permute-start.4) | collective-permute-done | bytes 24608 | tf_op jit(solution)/shard_map/ppermute | solution.py:31
  21.8 1.7 %conv.1 = (bf16[4,320,768]{2,1,0:T(8,128)(2,1)S(1)}, f32[1024,128]{1,0:T(8,128)S(1)}, f32[8,128]{1,0:T(8,128)S(1)}, f32[8,768]{1,0:T(8,128)S(1)}) custom-call(f32[8,768]{1,0:T(8,128)S(1)} %add.41.refs_0_, bf16[4,256,768]{2,1,0:T(8,128)(2,1)S(1)} %copy-done, bf16[4,32,768]{2,1,0:T(8,128)(2,1)S(1)} %collective-permute-done.2.refs_2_, ...), custom_call_target="tpu_custom_call" | custom-call | flops 754974720 | bytes 5109760 | tf_op jit(solution)/shard_map/conv/pallas_call | solution.py:665
  23.5 1.2 %collective-permute-done.5 = f32[8,128]{1,0:T(8,128)S(1)} collective-permute-done((f32[8,128]{1,0:T(8,128)S(1)}, f32[8,128]{1,0:T(8,128)S(1)}, u32[]{:S(2)}, u32[]{:S(2)}) %collective-permute-start.5) | collective-permute-done | bytes 4128 | tf_op jit(solution)/shard_map/ppermute | solution.py:31
  24.7 3.3 %collective-permute-start.8 = (f32[8,128]{1,0:T(8,128)S(1)}, f32[8,128]{1,0:T(8,128)S(1)}, u32[]{:S(2)}, u32[]{:S(2)}) collective-permute-start(f32[8,128]{1,0:T(8,128)S(1)} %add.42.refs_0_), channel_id=1, source_target_pairs={{0,24},{8,16},{16,8},{24,0},{1,25},{9,17},{17,9},{25,1},{2,26},{10... | collective-permute-start | bytes 12296 | tf_op jit(solution)/shard_map/ppermute | solution.py:31
  27.9 1.1 %collective-permute-start.6 = (f32[8,128]{1,0:T(8,128)S(1)}, f32[8,128]{1,0:T(8,128)S(1)}, u32[]{:S(2)}, u32[]{:S(2)}) collective-permute-start(f32[8,128]{1,0:T(8,128)S(1)} %add.42.refs_0_), channel_id=1, source_target_pairs={{0,8},{8,0},{16,24},{24,16},{1,9},{9,1},{17,25},{25,17},{2,10},{10... | collective-permute-start | bytes 12296 | tf_op jit(solution)/shard_map/ppermute | solution.py:31
  29.1 0.6 back.1.refs_7_
  29.7 0.4 collective-permute-done.8.refs_3_
  30.1 2.4 %collective-permute-done.7.refs_2_ = f32[8,128]{1,0:T(8,128)S(1)} collective-permute-done((f32[8,128]{1,0:T(8,128)S(1)}, f32[8,128]{1,0:T(8,128)S(1)}, u32[]{:S(2)}, u32[]{:S(2)}) %collective-permute-start.7) | collective-permute-done | bytes 4128 | tf_op jit(solution)/shard_map/ppermute | solution.py:31
  32.5 0.6 collective-permute-start.16
  33.1 0.5 collective-permute-start.17
  33.6 0.4 mix.1
  34.1 1.2 %collective-permute-done.11 = f32[8,128]{1,0:T(8,128)S(1)} collective-permute-done((f32[8,128]{1,0:T(8,128)S(1)}, f32[8,128]{1,0:T(8,128)S(1)}, u32[]{:S(2)}, u32[]{:S(2)}) %collective-permute-start.11) | collective-permute-done | bytes 4128 | tf_op jit(solution)/shard_map/ppermute | solution.py:31
  35.3 1.7 %collective-permute-start.14 = (f32[8,128]{1,0:T(8,128)S(1)}, f32[8,128]{1,0:T(8,128)S(1)}, u32[]{:S(2)}, u32[]{:S(2)}) collective-permute-start(f32[8,128]{1,0:T(8,128)S(1)} %add.43.refs_0_), channel_id=1, source_target_pairs={{0,24},{8,16},{16,8},{24,0},{1,25},{9,17},{17,9},{25,1},{2,26},{10... | collective-permute-start | bytes 12296 | tf_op jit(solution)/shard_map/ppermute | solution.py:31
  37.3 2.4 %collective-permute-start.12 = (f32[8,128]{1,0:T(8,128)S(1)}, f32[8,128]{1,0:T(8,128)S(1)}, u32[]{:S(2)}, u32[]{:S(2)}) collective-permute-start(f32[8,128]{1,0:T(8,128)S(1)} %add.43.refs_0_), channel_id=1, source_target_pairs={{0,8},{8,0},{16,24},{24,16},{1,9},{9,1},{17,25},{25,17},{2,10},{10... | collective-permute-start | bytes 12296 | tf_op jit(solution)/shard_map/ppermute | solution.py:31
  39.7 1.0 collective-permute-done.14.refs_3_
  40.7 0.8 collective-permute-done.13.refs_2_
  41.5 1.6 %grads.1 = (f32[96,1536]{1,0:T(8,128)S(1)}, bf16[96,1536]{1,0:T(8,128)(2,1)S(1)}, bf16[1024,128]{1,0:T(8,128)(2,1)S(1)}, bf16[4,32,128]{2,1,0:T(8,128)(2,1)S(1)}, bf16[4,32,128]{2,1,0:T(8,128)(2,1)S(1)}) custom-call(f32[8,128]{1,0:T(8,128)S(1)} %add.43.refs_0_, f32[8,128]{1,0:T(8,128)S(1)} %collective-permute-done.12.refs_1_, ...), custom_call_target="tpu_custom_call" | custom-call | flops 754974720 | bytes 6087680 | tf_op jit(solution)/shard_map/grads/pallas_call | solution.py:665
  43.3 1.6 %collective-permute-start.22 = (bf16[1536,128]{1,0:T(8,128)(2,1)S(1)}, bf16[1536,128]{1,0:T(8,128)(2,1)S(1)}, u32[]{:S(2)}, u32[]{:S(2)}) collective-permute-start(bf16[1536,128]{1,0:T(8,128)(2,1)S(1)} %both.1.refs_0_), channel_id=1, source_target_pairs={{0,4},{2,6},{4,0},{6,2},{1,5},{3,7},{5,1},{7,3},{8,12},{10,14},{12... | collective-permute-start | bytes 1179656 | tf_op jit(solution)/shard_map/ppermute | solution.py:31
  44.9 1.5 %collective-permute-start.21 = (bf16[1536,128]{1,0:T(8,128)(2,1)S(1)}, bf16[1536,128]{1,0:T(8,128)(2,1)S(1)}, u32[]{:S(2)}, u32[]{:S(2)}) collective-permute-start(bf16[1536,128]{1,0:T(8,128)(2,1)S(1)} %both.1.refs_0_), channel_id=1, source_target_pairs={{0,2},{2,0},{4,6},{6,4},{1,3},{3,1},{5,7},{7,5},{8,10},{10,8},{12,... | collective-permute-start | bytes 1179656 | tf_op jit(solution)/shard_map/ppermute | solution.py:31
  46.5 1.9 %collective-permute-start.18 = (bf16[144,384]{1,0:T(8,128)(2,1)S(1)}, bf16[144,384]{1,0:T(8,128)(2,1)S(1)}, u32[]{:S(2)}, u32[]{:S(2)}) collective-permute-start(bf16[144,384]{1,0:T(8,128)(2,1)S(1)} %get-tuple-element.141), channel_id=1, source_target_pairs={{0,8},{8,0},{16,24},{24,16},{1,9},{9,1},{17,25},{25,17},{2,10},{10... | collective-permute-start | bytes 331784 | tf_op jit(solution)/shard_map/ppermute | solution.py:31
  48.4 1.7 %collective-permute-start.20 = (bf16[144,384]{1,0:T(8,128)(2,1)S(1)}, bf16[144,384]{1,0:T(8,128)(2,1)S(1)}, u32[]{:S(2)}, u32[]{:S(2)}) collective-permute-start(bf16[144,384]{1,0:T(8,128)(2,1)S(1)} %get-tuple-element.143), channel_id=1, source_target_pairs={{0,24},{8,16},{16,8},{24,0},{1,25},{9,17},{17,9},{25,1},{2,26},{10... | collective-permute-start | bytes 331784 | tf_op jit(solution)/shard_map/ppermute | solution.py:31
  50.1 4.8 %collective-permute-done.22.refs_2_ = bf16[1536,128]{1,0:T(8,128)(2,1)S(1)} collective-permute-done((bf16[1536,128]{1,0:T(8,128)(2,1)S(1)}, bf16[1536,128]{1,0:T(8,128)(2,1)S(1)}, u32[]{:S(2)}, u32[]{:S(2)}) %collective-permute-start.22) | collective-permute-done | bytes 393248 | tf_op jit(solution)/shard_map/ppermute | solution.py:31
  54.9 1.2 %collective-permute-done.21.refs_1_ = bf16[1536,128]{1,0:T(8,128)(2,1)S(1)} collective-permute-done((bf16[1536,128]{1,0:T(8,128)(2,1)S(1)}, bf16[1536,128]{1,0:T(8,128)(2,1)S(1)}, u32[]{:S(2)}, u32[]{:S(2)}) %collective-permute-start.21) | collective-permute-done | bytes 393248 | tf_op jit(solution)/shard_map/ppermute | solution.py:31
  56.1 2.2 %collective-permute-done.19.refs_2_ = bf16[96,384]{1,0:T(8,128)(2,1)S(1)} collective-permute-done((bf16[96,384]{1,0:T(8,128)(2,1)S(1)}, bf16[96,384]{1,0:T(8,128)(2,1)S(1)}, u32[]{:S(2)}, u32[]{:S(2)}) %collective-permute-start.19) | collective-permute-done | bytes 73760 | tf_op jit(solution)/shard_map/ppermute | solution.py:31
  58.5 1.0 collective-permute-start.30
  59.5 2.2 %collective-permute-start.25 = (bf16[96,384]{1,0:T(8,128)(2,1)S(1)}, bf16[96,384]{1,0:T(8,128)(2,1)S(1)}, u32[]{:S(2)}, u32[]{:S(2)}) collective-permute-start(bf16[96,384]{1,0:T(8,128)(2,1)S(1)} %get-tuple-element.159.refs_0_), channel_id=1, source_target_pairs={{0,24},{8,16},{16,8},{24,0},{1,25},{9,17},{17,9},{25,1},{2,26},{10... | collective-permute-start | bytes 221192 | tf_op jit(solution)/shard_map/ppermute | solution.py:31
  61.7 2.2 %collective-permute-start.23 = (bf16[96,384]{1,0:T(8,128)(2,1)S(1)}, bf16[96,384]{1,0:T(8,128)(2,1)S(1)}, u32[]{:S(2)}, u32[]{:S(2)}) collective-permute-start(bf16[96,384]{1,0:T(8,128)(2,1)S(1)} %get-tuple-element.159.refs_0_), channel_id=1, source_target_pairs={{0,8},{8,0},{16,24},{24,16},{1,9},{9,1},{17,25},{25,17},{2,10},{10... | collective-permute-start | bytes 221192 | tf_op jit(solution)/shard_map/ppermute | solution.py:31
  63.9 0.4 fill.1.weight_ref
  64.3 2.1 %collective-permute-start.33 = (bf16[256,128]{1,0:T(8,128)(2,1)S(1)}, bf16[256,128]{1,0:T(8,128)(2,1)S(1)}, u32[]{:S(2)}, u32[]{:S(2)}) collective-permute-start(bf16[256,128]{1,0:T(8,128)(2,1)S(1)} %edges.1.refs_4_), channel_id=1, source_target_pairs={{0,6},{2,4},{4,2},{6,0},{1,7},{3,5},{5,3},{7,1},{8,14},{10,12},{12... | collective-permute-start | bytes 196616 | tf_op jit(solution)/shard_map/ppermute | solution.py:31
  66.5 1.1 %collective-permute-start.32 = (bf16[256,128]{1,0:T(8,128)(2,1)S(1)}, bf16[256,128]{1,0:T(8,128)(2,1)S(1)}, u32[]{:S(2)}, u32[]{:S(2)}) collective-permute-start(bf16[256,128]{1,0:T(8,128)(2,1)S(1)} %edges.1.refs_4_), channel_id=1, source_target_pairs={{0,4},{2,6},{4,0},{6,2},{1,5},{3,7},{5,1},{7,3},{8,12},{10,14},{12... | collective-permute-start | bytes 196616 | tf_op jit(solution)/shard_map/ppermute | solution.py:31
  67.6 1.2 %collective-permute-done.24.refs_2_ = bf16[96,384]{1,0:T(8,128)(2,1)S(1)} collective-permute-done((bf16[96,384]{1,0:T(8,128)(2,1)S(1)}, bf16[96,384]{1,0:T(8,128)(2,1)S(1)}, u32[]{:S(2)}, u32[]{:S(2)}) %collective-permute-start.24) | collective-permute-done | bytes 73760 | tf_op jit(solution)/shard_map/ppermute | solution.py:31
  68.8 1.1 %collective-permute-start.31 = (bf16[256,128]{1,0:T(8,128)(2,1)S(1)}, bf16[256,128]{1,0:T(8,128)(2,1)S(1)}, u32[]{:S(2)}, u32[]{:S(2)}) collective-permute-start(bf16[256,128]{1,0:T(8,128)(2,1)S(1)} %edges.1.refs_4_), channel_id=1, source_target_pairs={{0,2},{2,0},{4,6},{6,4},{1,3},{3,1},{5,7},{7,5},{8,10},{10,8},{12,... | collective-permute-start | bytes 196616 | tf_op jit(solution)/shard_map/ppermute | solution.py:31
  69.9 1.6 %collective-permute-start.29 = (bf16[96,1536]{1,0:T(8,128)(2,1)S(1)}, bf16[96,1536]{1,0:T(8,128)(2,1)S(1)}, u32[]{:S(2)}, u32[]{:S(2)}) collective-permute-start(bf16[96,1536]{1,0:T(8,128)(2,1)S(1)} %place.1.half_ref.refs_5_), channel_id=1, source_target_pairs={{0,6},{2,4},{4,2},{6,0},{1,7},{3,5},{5,3},{7,1},{8,14},{10,12},{12... | collective-permute-start | bytes 884744 | tf_op jit(solution)/shard_map/ppermute | solution.py:31
  71.5 0.9 collective-permute-start.28
  72.4 0.4 collective-permute-done.33.refs_7_
  72.8 0.7 collective-permute-start.27
  73.5 1.4 %collective-permute-done.32.refs_6_ = bf16[256,128]{1,0:T(8,128)(2,1)S(1)} collective-permute-done((bf16[256,128]{1,0:T(8,128)(2,1)S(1)}, bf16[256,128]{1,0:T(8,128)(2,1)S(1)}, u32[]{:S(2)}, u32[]{:S(2)}) %collective-permute-start.32) | collective-permute-done | bytes 65568 | tf_op jit(solution)/shard_map/ppermute | solution.py:31
  74.8 4.2 %tail.1 = (f32[4,256,768]{2,1,0:T(8,128)S(1)}, f32[8,768]{1,0:T(8,128)S(1)}) custom-call(bf16[4,256,768]{2,1,0:T(8,128)(2,1)S(1)} %copy-done, bf16[4,256,768]{2,1,0:T(8,128)(2,1)S(1)} %copy-done.1, f32[8,768]{1,0:T(8,128)S(1)} %get-tuple-element.123.refs_4_.stat_ref, bf16[4,512,768]{2,1,0:T(8,128)(2,1)S(1)} %fill.1.weight_ref, ...), custom_call_target="tpu_custom_call" | custom-call | flops 2415919104 | bytes 11321344 | tf_op jit(solution)/shard_map/tail/pallas_call | solution.py:665
  79.1 0.5 collective-permute-start.36
  79.6 0.6 multiply_subtract_fusion
  80.4 2.3 %branch.1 = bf16[4,256,768]{2,1,0:T(8,128)(2,1)} custom-call(bf16[4,256,768]{2,1,0:T(8,128)(2,1)S(1)} %copy-done, bf16[4,512,768]{2,1,0:T(8,128)(2,1)S(1)} %fill.1.weight_ref, bf16[1536,128]{1,0:T(8,128)(2,1)S(1)} %both.1.refs_0_, bf16[1536,128]{1,0:T(8,128)(2,1)S(1)} %collective-permute-done.21.refs_1_, ...), custom_call_target="tpu_custom_call" | custom-call | flops 805306368 | bytes 7864320 | tf_op jit(solution)/shard_map/branch/pallas_call | solution.py:665
  82.7 1.5 %collective-permute-done.35 = f32[8,768]{1,0:T(8,128)S(1)} collective-permute-done((f32[8,768]{1,0:T(8,128)S(1)}, f32[8,768]{1,0:T(8,128)S(1)}, u32[]{:S(2)}, u32[]{:S(2)}) %collective-permute-start.35) | collective-permute-done | bytes 24608 | tf_op jit(solution)/shard_map/ppermute | solution.py:31
  84.3 1.4 %moment.1 = (f32[96,2304]{1,0:T(8,128)}, f32[96,768]{1,0:T(8,128)}) custom-call(bf16[96,1536]{1,0:T(8,128)(2,1)S(1)} %place.1.half_ref.refs_5_, bf16[96,1536]{1,0:T(8,128)(2,1)S(1)} %collective-permute-done.36.other_ref, f32[96,2304]{1,0:T(8,128)S(1)} %bitcast.9, f32[96,768]{1,0:T(8,128)S(1)} %copy-done.4), custom_call_target="tpu_custom_call" | custom-call | flops 589824 | bytes 2949120 | tf_op jit(solution)/shard_map/moment/pallas_call | solution.py:665
  85.6 0.8 collective-permute-done.28.refs_7_
  86.4 0.9 gram_left.1
  87.4 0.7 collective-permute-start.38
  88.1 0.9 gram_right.1
  89.0 0.4 collective-permute-done.37.other_ref
  89.4 8.5 %newton.1.own_ref = f32[96,384]{1,0:T(8,128)S(1)} custom-call(f32[384,384]{1,0:T(8,128)S(1)} %get-tuple-element.180.left_ref, f32[384,384]{1,0:T(8,128)S(1)} %get-tuple-element.181.right_ref, f32[384,384]{1,0:T(8,128)S(1)} %collective-permute-done.37.other_ref), custom_call_target="tpu_custom_call" | custom-call | flops 5662310400 | bytes 1916928 | tf_op jit(solution)/shard_map/newton/pallas_call | solution.py:665
  98.1 0.4 right.1.right_ref
  98.6 0.5 collective-permute-start.41
  99.0 1.3 %input_grad.1 = (f32[4,256,768]{2,1,0:T(8,128)}, f32[2,768]{1,0:T(2,128)}, f32[2,768]{1,0:T(2,128)}) custom-call(f32[8,768]{1,0:T(8,128)S(1)} %add.50.total_ref, f32[4,256,768]{2,1,0:T(8,128)S(1)} %get-tuple-element.183.grad_ref, bf16[4,256,768]{2,1,0:T(8,128)(2,1)S(1)} %copy-done, f32[8,768]{1,0:T(8,128)S(1)} %get-tuple-element.123.refs_4_.stat_ref, ...), custom_call_target="tpu_custom_call" | custom-call | flops 3932160 | bytes 7942144 | tf_op jit(solution)/shard_map/input_grad/pallas_call | solution.py:665
  100.4 0.5 left.1.left_ref
  101.1 1.3 %input_grad_rest.1 = f32[4,256,768]{2,1,0:T(8,128)} custom-call(f32[8,768]{1,0:T(8,128)S(1)} %add.50.total_ref, f32[4,256,768]{2,1,0:T(8,128)S(1)} %get-tuple-element.183.grad_ref, bf16[4,256,768]{2,1,0:T(8,128)(2,1)S(1)} %copy-done, f32[8,768]{1,0:T(8,128)S(1)} %get-tuple-element.123.refs_4_.stat_ref, ...), custom_call_target="tpu_custom_call", output_to_operand_aliasing={{}: (5, {})} | custom-call | flops 3932160 | bytes 11063296 | tf_op jit(solution)/shard_map/input_grad_rest/pallas_call | solution.py:665
  102.4 1.3 %finish.1 = (f32[96,2304]{1,0:T(8,128)}, bf16[96,2304]{1,0:T(8,128)(2,1)}, f32[96,768]{1,0:T(8,128)}, bf16[96,768]{1,0:T(8,128)(2,1)}) custom-call(bf16[96,768]{1,0:T(8,128)(2,1)S(1)} %left.1.left_ref, bf16[96,768]{1,0:T(8,128)(2,1)S(1)} %right.1.right_ref, bf16[96,768]{1,0:T(8,128)(2,1)S(1)} %collective-permute-done.40.left_other, ...), custom_call_target="tpu_custom_call" | custom-call | flops 589824 | bytes 3538944 | tf_op jit(solution)/shard_map/finish/pallas_call | solution.py:665
  (78 shorter events, 2.1 us)
Async XLA Ops:
  0.6 21.1 %copy-start = (bf16[4,256,768]{2,1,0:T(8,128)(2,1)S(1)}, bf16[4,256,768]{2,1,0:T(8,128)(2,1)}, u32[]{:S(2)}) copy-start(bf16[4,256,768]{2,1,0:T(8,128)(2,1)} %x_ref.7) | copy-start | bytes 4718596
  0.7 21.1 %copy-start.6 = (s32[4,256]{1,0:T(4,128)S(1)}, s32[4,256]{1,0:T(4,128)}, u32[]{:S(2)}) copy-start(s32[4,256]{1,0:T(4,128)} %valid_ref.3) | copy-start | bytes 12292
  0.7 21.1 %copy-start.7 = (f32[2,768]{1,0:T(2,128)S(1)}, f32[2,768]{1,0:T(2,128)}, u32[]{:S(2)}) copy-start(f32[2,768]{1,0:T(2,128)} %refs_0_.1) | copy-start | bytes 18436
  0.7 28.4 %copy-start.1 = (bf16[4,256,768]{2,1,0:T(8,128)(2,1)S(1)}, bf16[4,256,768]{2,1,0:T(8,128)(2,1)}, u32[]{:S(2)}) copy-start(bf16[4,256,768]{2,1,0:T(8,128)(2,1)} %upstream_ref.1) | copy-start | bytes 4718596
  2.9 2.3 %collective-permute-start = (f32[8,768]{1,0:T(8,128)S(1)}, f32[8,768]{1,0:T(8,128)S(1)}, u32[]{:S(2)}, u32[]{:S(2)}) collective-permute-start(f32[8,768]{1,0:T(8,128)S(1)} %get-tuple-element.107.after_ref), channel_id=1, source_target_pairs={{0,1},{1,0},{2,3},{3,2},{4,5},{5,4},{6,7},{7,6},{8,9},{9,8},{10,11... | collective-permute-start | bytes 73736 | tf_op jit(solution)/shard_map/ppermute | solution.py:31
  5.2 27.2 %collective-permute-start.10 = (bf16[96,4608]{1,0:T(8,128)(2,1)S(1)}, bf16[96,4608]{1,0:T(8,128)(2,1)S(1)}, u32[]{:S(2)}, u32[]{:S(2)}) collective-permute-start(bf16[96,4608]{1,0:T(8,128)(2,1)S(1)} %get-tuple-element.117.refs_0_), channel_id=1, source_target_pairs={{0,4},{2,6},{4,0},{6,2},{1,5},{3,7},{5,1},{7,3},{8,12},{10,14},{12... | collective-permute-start | bytes 2654216 | tf_op jit(solution)/shard_map/ppermute | solution.py:31
  7.8 24.6 %collective-permute-start.9 = (bf16[96,4608]{1,0:T(8,128)(2,1)S(1)}, bf16[96,4608]{1,0:T(8,128)(2,1)S(1)}, u32[]{:S(2)}, u32[]{:S(2)}) collective-permute-start(bf16[96,4608]{1,0:T(8,128)(2,1)S(1)} %get-tuple-element.117.refs_0_), channel_id=1, source_target_pairs={{0,2},{2,0},{4,6},{6,4},{1,3},{3,1},{5,7},{7,5},{8,10},{10,8},{12,... | collective-permute-start | bytes 2654216 | tf_op jit(solution)/shard_map/ppermute | solution.py:31
  9.3 7.3 %collective-permute-start.2 = (bf16[4,32,768]{2,1,0:T(8,128)(2,1)S(1)}, bf16[4,32,768]{2,1,0:T(8,128)(2,1)S(1)}, u32[]{:S(2)}, u32[]{:S(2)}) collective-permute-start(bf16[4,32,768]{2,1,0:T(8,128)(2,1)S(1)} %get-tuple-element.110), channel_id=1, source_target_pairs={{0,8},{1,9},{8,0},{9,1},{16,24},{17,25},{24,16},{25,17},{2,10},{3,... | collective-permute-start | bytes 589832 | tf_op jit(solution)/shard_map/ppermute | solution.py:82
  10.9 5.7 %collective-permute-start.3 = (bf16[4,32,768]{2,1,0:T(8,128)(2,1)S(1)}, bf16[4,32,768]{2,1,0:T(8,128)(2,1)S(1)}, u32[]{:S(2)}, u32[]{:S(2)}) collective-permute-start(bf16[4,32,768]{2,1,0:T(8,128)(2,1)S(1)} %get-tuple-element.111), channel_id=1, source_target_pairs={{0,1},{1,0},{8,16},{9,17},{16,8},{17,9},{24,25},{25,24},{2,3},{3,2... | collective-permute-start | bytes 589832 | tf_op jit(solution)/shard_map/ppermute | solution.py:82
  10.9 5.7 %collective-permute-start.1 = (f32[8,768]{1,0:T(8,128)S(1)}, f32[8,768]{1,0:T(8,128)S(1)}, u32[]{:S(2)}, u32[]{:S(2)}) collective-permute-start(f32[8,768]{1,0:T(8,128)S(1)} %add.39), channel_id=1, source_target_pairs={{0,8},{8,0},{16,24},{24,16},{1,9},{9,1},{17,25},{25,17},{2,10},{10... | collective-permute-start | bytes 73736 | tf_op jit(solution)/shard_map/ppermute | solution.py:31
  16.6 5.1 %collective-permute-start.4 = (f32[8,768]{1,0:T(8,128)S(1)}, f32[8,768]{1,0:T(8,128)S(1)}, u32[]{:S(2)}, u32[]{:S(2)}) collective-permute-start(f32[8,768]{1,0:T(8,128)S(1)} %add.40), channel_id=1, source_target_pairs={{0,16},{8,24},{16,0},{24,8},{1,17},{9,25},{17,1},{25,9},{2,18},{10... | collective-permute-start | bytes 73736 | tf_op jit(solution)/shard_map/ppermute | solution.py:31
  21.8 11.9 %copy-start.9 = (f32[2,96]{1,0:T(2,128)S(1)}, f32[2,96]{1,0:T(2,128)}, u32[]{:S(2)}) copy-start(f32[2,96]{1,0:T(2,128)} %param.20) | copy-start | bytes 2308
  23.5 1.2 %collective-permute-start.5 = (f32[8,128]{1,0:T(8,128)S(1)}, f32[8,128]{1,0:T(8,128)S(1)}, u32[]{:S(2)}, u32[]{:S(2)}) collective-permute-start(f32[8,128]{1,0:T(8,128)S(1)} %get-tuple-element.116), channel_id=1, source_target_pairs={{0,1},{1,0},{2,3},{3,2},{4,5},{5,4},{6,7},{7,6},{8,9},{9,8},{10,11... | collective-permute-start | bytes 12296 | tf_op jit(solution)/shard_map/ppermute | solution.py:31
  24.7 5.4 %collective-permute-start.8 = (f32[8,128]{1,0:T(8,128)S(1)}, f32[8,128]{1,0:T(8,128)S(1)}, u32[]{:S(2)}, u32[]{:S(2)}) collective-permute-start(f32[8,128]{1,0:T(8,128)S(1)} %add.42.refs_0_), channel_id=1, source_target_pairs={{0,24},{8,16},{16,8},{24,0},{1,25},{9,17},{17,9},{25,1},{2,26},{10... | collective-permute-start | bytes 12296 | tf_op jit(solution)/shard_map/ppermute | solution.py:31
  27.9 4.5 %collective-permute-start.7 = (f32[8,128]{1,0:T(8,128)S(1)}, f32[8,128]{1,0:T(8,128)S(1)}, u32[]{:S(2)}, u32[]{:S(2)}) collective-permute-start(f32[8,128]{1,0:T(8,128)S(1)} %add.42.refs_0_), channel_id=1, source_target_pairs={{0,16},{8,24},{16,0},{24,8},{1,17},{9,25},{17,1},{25,9},{2,18},{10... | collective-permute-start | bytes 12296 | tf_op jit(solution)/shard_map/ppermute | solution.py:31
  27.9 4.5 %collective-permute-start.6 = (f32[8,128]{1,0:T(8,128)S(1)}, f32[8,128]{1,0:T(8,128)S(1)}, u32[]{:S(2)}, u32[]{:S(2)}) collective-permute-start(f32[8,128]{1,0:T(8,128)S(1)} %add.42.refs_0_), channel_id=1, source_target_pairs={{0,8},{8,0},{16,24},{24,16},{1,9},{9,1},{17,25},{25,17},{2,10},{10... | collective-permute-start | bytes 12296 | tf_op jit(solution)/shard_map/ppermute | solution.py:31
  32.5 13.9 %collective-permute-start.16 = (bf16[96,2304]{1,0:T(8,128)(2,1)S(1)}, bf16[96,2304]{1,0:T(8,128)(2,1)S(1)}, u32[]{:S(2)}, u32[]{:S(2)}) collective-permute-start(bf16[96,2304]{1,0:T(8,128)(2,1)S(1)} %get-tuple-element.135), channel_id=1, source_target_pairs={{0,4},{2,6},{4,0},{6,2},{1,5},{3,7},{5,1},{7,3},{8,12},{10,14},{12... | collective-permute-start | bytes 1327112 | tf_op jit(solution)/shard_map/ppermute | solution.py:31
  33.1 13.3 %collective-permute-start.17 = (bf16[96,2304]{1,0:T(8,128)(2,1)S(1)}, bf16[96,2304]{1,0:T(8,128)(2,1)S(1)}, u32[]{:S(2)}, u32[]{:S(2)}) collective-permute-start(bf16[96,2304]{1,0:T(8,128)(2,1)S(1)} %get-tuple-element.136), channel_id=1, source_target_pairs={{0,2},{2,0},{4,6},{6,4},{1,3},{3,1},{5,7},{7,5},{8,10},{10,8},{12,... | collective-permute-start | bytes 1327112 | tf_op jit(solution)/shard_map/ppermute | solution.py:31
  34.0 1.2 %collective-permute-start.11 = (f32[8,128]{1,0:T(8,128)S(1)}, f32[8,128]{1,0:T(8,128)S(1)}, u32[]{:S(2)}, u32[]{:S(2)}) collective-permute-start(f32[8,128]{1,0:T(8,128)S(1)} %get-tuple-element.126), channel_id=1, source_target_pairs={{0,1},{1,0},{2,3},{3,2},{4,5},{5,4},{6,7},{7,6},{8,9},{9,8},{10,11... | collective-permute-start | bytes 12296 | tf_op jit(solution)/shard_map/ppermute | solution.py:31
  35.3 5.4 %collective-permute-start.14 = (f32[8,128]{1,0:T(8,128)S(1)}, f32[8,128]{1,0:T(8,128)S(1)}, u32[]{:S(2)}, u32[]{:S(2)}) collective-permute-start(f32[8,128]{1,0:T(8,128)S(1)} %add.43.refs_0_), channel_id=1, source_target_pairs={{0,24},{8,16},{16,8},{24,0},{1,25},{9,17},{17,9},{25,1},{2,26},{10... | collective-permute-start | bytes 12296 | tf_op jit(solution)/shard_map/ppermute | solution.py:31
  37.0 4.5 %collective-permute-start.13 = (f32[8,128]{1,0:T(8,128)S(1)}, f32[8,128]{1,0:T(8,128)S(1)}, u32[]{:S(2)}, u32[]{:S(2)}) collective-permute-start(f32[8,128]{1,0:T(8,128)S(1)} %add.43.refs_0_), channel_id=1, source_target_pairs={{0,16},{8,24},{16,0},{24,8},{1,17},{9,25},{17,1},{25,9},{2,18},{10... | collective-permute-start | bytes 12296 | tf_op jit(solution)/shard_map/ppermute | solution.py:31
  37.3 4.2 %collective-permute-start.12 = (f32[8,128]{1,0:T(8,128)S(1)}, f32[8,128]{1,0:T(8,128)S(1)}, u32[]{:S(2)}, u32[]{:S(2)}) collective-permute-start(f32[8,128]{1,0:T(8,128)S(1)} %add.43.refs_0_), channel_id=1, source_target_pairs={{0,8},{8,0},{16,24},{24,16},{1,9},{9,1},{17,25},{25,17},{2,10},{10... | collective-permute-start | bytes 12296 | tf_op jit(solution)/shard_map/ppermute | solution.py:31
  43.0 3.4 %collective-permute-start.15 = (bf16[96,1536]{1,0:T(8,128)(2,1)S(1)}, bf16[96,1536]{1,0:T(8,128)(2,1)S(1)}, u32[]{:S(2)}, u32[]{:S(2)}) collective-permute-start(bf16[96,1536]{1,0:T(8,128)(2,1)S(1)} %get-tuple-element.132), channel_id=1, source_target_pairs={{0,1},{1,0},{2,3},{3,2},{4,5},{5,4},{6,7},{7,6},{8,9},{9,8},{10,11... | collective-permute-start | bytes 884744 | tf_op jit(solution)/shard_map/ppermute | solution.py:31
  43.3 11.6 %collective-permute-start.22 = (bf16[1536,128]{1,0:T(8,128)(2,1)S(1)}, bf16[1536,128]{1,0:T(8,128)(2,1)S(1)}, u32[]{:S(2)}, u32[]{:S(2)}) collective-permute-start(bf16[1536,128]{1,0:T(8,128)(2,1)S(1)} %both.1.refs_0_), channel_id=1, source_target_pairs={{0,4},{2,6},{4,0},{6,2},{1,5},{3,7},{5,1},{7,3},{8,12},{10,14},{12... | collective-permute-start | bytes 1179656 | tf_op jit(solution)/shard_map/ppermute | solution.py:31
  44.9 11.2 %collective-permute-start.21 = (bf16[1536,128]{1,0:T(8,128)(2,1)S(1)}, bf16[1536,128]{1,0:T(8,128)(2,1)S(1)}, u32[]{:S(2)}, u32[]{:S(2)}) collective-permute-start(bf16[1536,128]{1,0:T(8,128)(2,1)S(1)} %both.1.refs_0_), channel_id=1, source_target_pairs={{0,2},{2,0},{4,6},{6,4},{1,3},{3,1},{5,7},{7,5},{8,10},{10,8},{12,... | collective-permute-start | bytes 1179656 | tf_op jit(solution)/shard_map/ppermute | solution.py:31
  46.5 11.8 %collective-permute-start.18 = (bf16[144,384]{1,0:T(8,128)(2,1)S(1)}, bf16[144,384]{1,0:T(8,128)(2,1)S(1)}, u32[]{:S(2)}, u32[]{:S(2)}) collective-permute-start(bf16[144,384]{1,0:T(8,128)(2,1)S(1)} %get-tuple-element.141), channel_id=1, source_target_pairs={{0,8},{8,0},{16,24},{24,16},{1,9},{9,1},{17,25},{25,17},{2,10},{10... | collective-permute-start | bytes 331784 | tf_op jit(solution)/shard_map/ppermute | solution.py:31
  48.4 9.9 %collective-permute-start.20 = (bf16[144,384]{1,0:T(8,128)(2,1)S(1)}, bf16[144,384]{1,0:T(8,128)(2,1)S(1)}, u32[]{:S(2)}, u32[]{:S(2)}) collective-permute-start(bf16[144,384]{1,0:T(8,128)(2,1)S(1)} %get-tuple-element.143), channel_id=1, source_target_pairs={{0,24},{8,16},{16,8},{24,0},{1,25},{9,17},{17,9},{25,1},{2,26},{10... | collective-permute-start | bytes 331784 | tf_op jit(solution)/shard_map/ppermute | solution.py:31
  50.1 8.3 %collective-permute-start.19 = (bf16[96,384]{1,0:T(8,128)(2,1)S(1)}, bf16[96,384]{1,0:T(8,128)(2,1)S(1)}, u32[]{:S(2)}, u32[]{:S(2)}) collective-permute-start(bf16[96,384]{1,0:T(8,128)(2,1)S(1)} %get-tuple-element.142), channel_id=1, source_target_pairs={{0,16},{8,24},{16,0},{24,8},{1,17},{9,25},{17,1},{25,9},{2,18},{10... | collective-permute-start | bytes 221192 | tf_op jit(solution)/shard_map/ppermute | solution.py:31
  58.4 5.5 %collective-permute-start.26 = (bf16[288,1536]{1,0:T(8,128)(2,1)S(1)}, bf16[288,1536]{1,0:T(8,128)(2,1)S(1)}, u32[]{:S(2)}, u32[]{:S(2)}) collective-permute-start(bf16[288,1536]{1,0:T(8,128)(2,1)S(1)} %pack.1), channel_id=1, source_target_pairs={{0,1},{1,0},{2,3},{3,2},{4,5},{5,4},{6,7},{7,6},{8,9},{9,8},{10,11... | collective-permute-start | bytes 2654216 | tf_op jit(solution)/shard_map/ppermute | solution.py:31
  58.5 13.0 %collective-permute-start.30 = (bf16[1536,128]{1,0:T(8,128)(2,1)S(1)}, bf16[1536,128]{1,0:T(8,128)(2,1)S(1)}, u32[]{:S(2)}, u32[]{:S(2)}) collective-permute-start(bf16[1536,128]{1,0:T(8,128)(2,1)S(1)} %both.1.refs_0_), channel_id=1, source_target_pairs={{0,6},{2,4},{4,2},{6,0},{1,7},{3,5},{5,3},{7,1},{8,14},{10,12},{12... | collective-permute-start | bytes 1179656 | tf_op jit(solution)/shard_map/ppermute | solution.py:31
  59.5 7.0 %collective-permute-start.25 = (bf16[96,384]{1,0:T(8,128)(2,1)S(1)}, bf16[96,384]{1,0:T(8,128)(2,1)S(1)}, u32[]{:S(2)}, u32[]{:S(2)}) collective-permute-start(bf16[96,384]{1,0:T(8,128)(2,1)S(1)} %get-tuple-element.159.refs_0_), channel_id=1, source_target_pairs={{0,24},{8,16},{16,8},{24,0},{1,25},{9,17},{17,9},{25,1},{2,26},{10... | collective-permute-start | bytes 221192 | tf_op jit(solution)/shard_map/ppermute | solution.py:31
  61.7 7.1 %collective-permute-start.24 = (bf16[96,384]{1,0:T(8,128)(2,1)S(1)}, bf16[96,384]{1,0:T(8,128)(2,1)S(1)}, u32[]{:S(2)}, u32[]{:S(2)}) collective-permute-start(bf16[96,384]{1,0:T(8,128)(2,1)S(1)} %get-tuple-element.159.refs_0_), channel_id=1, source_target_pairs={{0,16},{8,24},{16,0},{24,8},{1,17},{9,25},{17,1},{25,9},{2,18},{10... | collective-permute-start | bytes 221192 | tf_op jit(solution)/shard_map/ppermute | solution.py:31
  61.7 8.1 %collective-permute-start.23 = (bf16[96,384]{1,0:T(8,128)(2,1)S(1)}, bf16[96,384]{1,0:T(8,128)(2,1)S(1)}, u32[]{:S(2)}, u32[]{:S(2)}) collective-permute-start(bf16[96,384]{1,0:T(8,128)(2,1)S(1)} %get-tuple-element.159.refs_0_), channel_id=1, source_target_pairs={{0,8},{8,0},{16,24},{24,16},{1,9},{9,1},{17,25},{25,17},{2,10},{10... | collective-permute-start | bytes 221192 | tf_op jit(solution)/shard_map/ppermute | solution.py:31
  64.3 8.5 %collective-permute-start.33 = (bf16[256,128]{1,0:T(8,128)(2,1)S(1)}, bf16[256,128]{1,0:T(8,128)(2,1)S(1)}, u32[]{:S(2)}, u32[]{:S(2)}) collective-permute-start(bf16[256,128]{1,0:T(8,128)(2,1)S(1)} %edges.1.refs_4_), channel_id=1, source_target_pairs={{0,6},{2,4},{4,2},{6,0},{1,7},{3,5},{5,3},{7,1},{8,14},{10,12},{12... | collective-permute-start | bytes 196616 | tf_op jit(solution)/shard_map/ppermute | solution.py:31
  66.5 8.3 %collective-permute-start.32 = (bf16[256,128]{1,0:T(8,128)(2,1)S(1)}, bf16[256,128]{1,0:T(8,128)(2,1)S(1)}, u32[]{:S(2)}, u32[]{:S(2)}) collective-permute-start(bf16[256,128]{1,0:T(8,128)(2,1)S(1)} %edges.1.refs_4_), channel_id=1, source_target_pairs={{0,4},{2,6},{4,0},{6,2},{1,5},{3,7},{5,1},{7,3},{8,12},{10,14},{12... | collective-permute-start | bytes 196616 | tf_op jit(solution)/shard_map/ppermute | solution.py:31
  68.8 6.1 %collective-permute-start.31 = (bf16[256,128]{1,0:T(8,128)(2,1)S(1)}, bf16[256,128]{1,0:T(8,128)(2,1)S(1)}, u32[]{:S(2)}, u32[]{:S(2)}) collective-permute-start(bf16[256,128]{1,0:T(8,128)(2,1)S(1)} %edges.1.refs_4_), channel_id=1, source_target_pairs={{0,2},{2,0},{4,6},{6,4},{1,3},{3,1},{5,7},{7,5},{8,10},{10,8},{12,... | collective-permute-start | bytes 196616 | tf_op jit(solution)/shard_map/ppermute | solution.py:31
  69.9 9.7 %copy-start.10 = (f32[2,96]{1,0:T(2,128)S(1)}, f32[2,96]{1,0:T(2,128)}, u32[]{:S(2)}) copy-start(f32[2,96]{1,0:T(2,128)} %param.21) | copy-start | bytes 2308
  69.9 15.7 %collective-permute-start.29 = (bf16[96,1536]{1,0:T(8,128)(2,1)S(1)}, bf16[96,1536]{1,0:T(8,128)(2,1)S(1)}, u32[]{:S(2)}, u32[]{:S(2)}) collective-permute-start(bf16[96,1536]{1,0:T(8,128)(2,1)S(1)} %place.1.half_ref.refs_5_), channel_id=1, source_target_pairs={{0,6},{2,4},{4,2},{6,0},{1,7},{3,5},{5,3},{7,1},{8,14},{10,12},{12... | collective-permute-start | bytes 884744 | tf_op jit(solution)/shard_map/ppermute | solution.py:31
  71.5 14.9 %collective-permute-start.28 = (bf16[96,1536]{1,0:T(8,128)(2,1)S(1)}, bf16[96,1536]{1,0:T(8,128)(2,1)S(1)}, u32[]{:S(2)}, u32[]{:S(2)}) collective-permute-start(bf16[96,1536]{1,0:T(8,128)(2,1)S(1)} %place.1.half_ref.refs_5_), channel_id=1, source_target_pairs={{0,4},{2,6},{4,0},{6,2},{1,5},{3,7},{5,1},{7,3},{8,12},{10,14},{12... | collective-permute-start | bytes 884744 | tf_op jit(solution)/shard_map/ppermute | solution.py:31
  72.8 13.6 %collective-permute-start.27 = (bf16[96,1536]{1,0:T(8,128)(2,1)S(1)}, bf16[96,1536]{1,0:T(8,128)(2,1)S(1)}, u32[]{:S(2)}, u32[]{:S(2)}) collective-permute-start(bf16[96,1536]{1,0:T(8,128)(2,1)S(1)} %place.1.half_ref.refs_5_), channel_id=1, source_target_pairs={{0,2},{2,0},{4,6},{6,4},{1,3},{3,1},{5,7},{7,5},{8,10},{10,8},{12,... | collective-permute-start | bytes 884744 | tf_op jit(solution)/shard_map/ppermute | solution.py:31
  79.1 1.3 %collective-permute-start.34 = (f32[8,768]{1,0:T(8,128)S(1)}, f32[8,768]{1,0:T(8,128)S(1)}, u32[]{:S(2)}, u32[]{:S(2)}) collective-permute-start(f32[8,768]{1,0:T(8,128)S(1)} %get-tuple-element.169), channel_id=1, source_target_pairs={{0,1},{1,0},{2,3},{3,2},{4,5},{5,4},{6,7},{7,6},{8,9},{9,8},{10,11... | collective-permute-start | bytes 73736 | tf_op jit(solution)/shard_map/ppermute | solution.py:31
  79.1 5.1 %collective-permute-start.36 = (bf16[96,1536]{1,0:T(8,128)(2,1)S(1)}, bf16[96,1536]{1,0:T(8,128)(2,1)S(1)}, u32[]{:S(2)}, u32[]{:S(2)}) collective-permute-start(bf16[96,1536]{1,0:T(8,128)(2,1)S(1)} %place.1.half_ref.refs_5_), channel_id=1, source_target_pairs={{0,1},{1,0},{2,3},{3,2},{4,5},{5,4},{6,7},{7,6},{8,9},{9,8},{10,11... | collective-permute-start | bytes 884744 | tf_op jit(solution)/shard_map/ppermute | solution.py:31
  80.3 3.9 %copy-start.2 = (f32[2304,96]{0,1:T(8,128)S(1)}, f32[2304,96]{0,1:T(8,128)}, u32[]{:S(2)}) copy-start(f32[2304,96]{0,1:T(8,128)} %param.15) | copy-start | bytes 2654212
  80.3 3.9 %copy-start.4 = (f32[96,768]{1,0:T(8,128)S(1)}, f32[96,768]{1,0:T(8,128)}, u32[]{:S(2)}) copy-start(f32[96,768]{1,0:T(8,128)} %two_ref.2) | copy-start | bytes 884740
  80.3 3.9 %collective-permute-start.35 = (f32[8,768]{1,0:T(8,128)S(1)}, f32[8,768]{1,0:T(8,128)S(1)}, u32[]{:S(2)}, u32[]{:S(2)}) collective-permute-start(f32[8,768]{1,0:T(8,128)S(1)} %add.44), channel_id=1, source_target_pairs={{0,8},{8,0},{16,24},{24,16},{1,9},{9,1},{17,25},{25,17},{2,10},{10... | collective-permute-start | bytes 73736 | tf_op jit(solution)/shard_map/ppermute | solution.py:31
  87.3 2.1 %collective-permute-start.37 = (f32[384,384]{1,0:T(8,128)S(1)}, f32[384,384]{1,0:T(8,128)S(1)}, u32[]{:S(2)}, u32[]{:S(2)}) collective-permute-start(f32[384,384]{1,0:T(8,128)S(1)} %get-tuple-element.180.left_ref), channel_id=1, source_target_pairs={{0,1},{1,0},{2,3},{3,2},{4,5},{5,4},{6,7},{7,6},{8,9},{9,8},{10,11... | collective-permute-start | bytes 1769480 | tf_op jit(solution)/shard_map/ppermute | solution.py:31
  87.4 10.5 %collective-permute-start.38 = (f32[8,768]{1,0:T(8,128)S(1)}, f32[8,768]{1,0:T(8,128)S(1)}, u32[]{:S(2)}, u32[]{:S(2)}) collective-permute-start(f32[8,768]{1,0:T(8,128)S(1)} %add.45), channel_id=1, source_target_pairs={{0,16},{8,24},{16,0},{24,8},{1,17},{9,25},{17,1},{25,9},{2,18},{10... | collective-permute-start | bytes 73736 | tf_op jit(solution)/shard_map/ppermute | solution.py:31
  89.4 9.6 %copy-start.8 = (f32[2,768]{1,0:T(2,128)S(1)}, f32[2,768]{1,0:T(2,128)}, u32[]{:S(2)}) copy-start(f32[2,768]{1,0:T(2,128)} %refs_1_.5) | copy-start | bytes 18436
  97.9 2.5 %collective-permute-start.39 = (f32[96,384]{1,0:T(8,128)S(1)}, f32[96,384]{1,0:T(8,128)S(1)}, u32[]{:S(2)}, u32[]{:S(2)}) collective-permute-start(f32[96,384]{1,0:T(8,128)S(1)} %newton.1.own_ref), channel_id=1, source_target_pairs={{0,1},{1,0},{2,3},{3,2},{4,5},{5,4},{6,7},{7,6},{8,9},{9,8},{10,11... | collective-permute-start | bytes 442376 | tf_op jit(solution)/shard_map/ppermute | solution.py:31
  98.6 3.8 %collective-permute-start.41 = (bf16[96,768]{1,0:T(8,128)(2,1)S(1)}, bf16[96,768]{1,0:T(8,128)(2,1)S(1)}, u32[]{:S(2)}, u32[]{:S(2)}) collective-permute-start(bf16[96,768]{1,0:T(8,128)(2,1)S(1)} %right.1.right_ref), channel_id=1, source_target_pairs={{0,1},{1,0},{2,3},{3,2},{4,5},{5,4},{6,7},{7,6},{8,9},{9,8},{10,11... | collective-permute-start | bytes 442376 | tf_op jit(solution)/shard_map/ppermute | solution.py:31
  100.9 1.6 %copy-start.3 = (f32[2304,96]{0,1:T(8,128)S(1)}, f32[2304,96]{0,1:T(8,128)}, u32[]{:S(2)}) copy-start(f32[2304,96]{0,1:T(8,128)} %param.14) | copy-start | bytes 2654212
  100.9 1.6 %copy-start.5 = (f32[96,768]{1,0:T(8,128)S(1)}, f32[96,768]{1,0:T(8,128)}, u32[]{:S(2)}) copy-start(f32[96,768]{1,0:T(8,128)} %two_ref.3) | copy-start | bytes 884740
  100.9 1.5 %collective-permute-start.40 = (bf16[96,768]{1,0:T(8,128)(2,1)S(1)}, bf16[96,768]{1,0:T(8,128)(2,1)S(1)}, u32[]{:S(2)}, u32[]{:S(2)}) collective-permute-start(bf16[96,768]{1,0:T(8,128)(2,1)S(1)} %left.1.left_ref), channel_id=1, source_target_pairs={{0,1},{1,0},{2,3},{3,2},{4,5},{5,4},{6,7},{7,6},{8,9},{9,8},{10,11... | collective-permute-start | bytes 442376 | tf_op jit(solution)/shard_map/ppermute | solution.py:31
